TPU v7x, 256 devices: a whole 4x4x8 slice. The times are simulated.
256 devices in a mesh: seq: 16 (over y, x_hi, core), blk: 16 (over z, x_lo).
Axes of the slice: x: 4 (x_hi: 2, x_lo: 2; x = x_hi * 2 + x_lo), y: 4, z: 8, core: 2. Of those that a mesh axis runs over, the one named last changes fastest.
Arguments:
- hidden_states: bfloat16 [16384, 4096], P(('seq', 'blk')), may hold values from -6 to 6
- query_weight: bfloat16 [4096, 4096], P(None, 'blk'), may hold values from -7.8125 to 7.8125
- kv_weight: bfloat16 [896, 2, 4096], P(None, None, 'blk'), may hold values from -0.1875 to 0.1875
- output_weight: bfloat16 [4096, 4096], P('blk'), may hold values from -0.09375 to 0.09375
- enc_in_weight: bfloat16 [3584, 896], P('blk'), may hold values from -0.1875 to 0.1875
- enc_out_weight: bfloat16 [3584, 896], P('blk'), may hold values from -0.09375 to 0.09375
- neighbours: bfloat16 [128, 768, 896], P('blk', 'seq'), may hold values from -6 to 6
- counts: int32 [16], replicated, may hold values from 1 to 48, 512 in all
- slot_of: int32 [512], replicated, may hold values from 0 to 511, as said below
Outputs:
- output: bfloat16 [16384, 4096], P(('seq', 'blk'))
Inputs may be any that keep to these rules, and one draw needn't show every extreme that they name: counts sum to 512 and the largest is exactly 48. slot_of is a permutation; the neighbours kept by one holder fill at most 3 slots of any one index of seq, and some holder reaches 3; each index of seq owns 32 slots.
All inputs are finite; a program needn't handle non-finite values.
Results may differ from a plain program's by a relative error of at most 0.027.
The roundings to bfloat16 on the way count: a program that leaves them out, or rounds other values in their place, can miss the bound.
Values may be sent and summed in bfloat16 or wider, within the bound.
No kernel may reach another device: no remote copies, remote signals or barrier semaphores. Data moves between devices by JAX's collectives and lax.ppermute only.
A program may use at most 128 MiB of HBM per device.

v0:
```python
import jax
import jax.numpy as jnp
from jax import lax
from jax.experimental import pallas as pl
from jax.experimental.pallas import tpu as pltpu
from jax.sharding import Mesh, PartitionSpec as P

HD = 128
CT = 64
K_NB = 2
EPS = 1e-06
AXES = ("y", "xh", "core", "z", "xl")
SIZES = (4, 2, 2, 8, 2)


def coords_of(index):
    out = []
    for size in reversed(SIZES):
        out.append(index % size)
        index //= size
    return tuple(reversed(out))


def index_of(coords):
    index = 0
    for size, coord in zip(SIZES, coords):
        index = index * size + coord % size
    return index


def pairs(target):
    count = index_of(tuple(s - 1 for s in SIZES)) + 1
    return [(i, index_of(target(*coords_of(i)))) for i in range(count)]


def x_shift(y, xh, core, z, xl, step):
    x = (xh * 2 + xl + step) % 4
    return (y, x // 2, core, z, x % 2)


X_OUT = pairs(lambda y, xh, c, z, xl: x_shift(y, xh, c, z, xl, 1 - 2 * c))
X_BACK = pairs(lambda y, xh, c, z, xl: x_shift(y, xh, c, z, xl, 2 * c - 1))
CORE = pairs(lambda y, xh, c, z, xl: (y, xh, 1 - c, z, xl))
Y_UP = [pairs(lambda y, xh, c, z, xl, d=d: (y + d, xh, c, z, xl)) for d in range(4)]
def steps_a(y, core):
    return (y, 4 if y == 0 else 8 - y)[core]


def steps_b(y, core):
    return ((4 - y) % 4, y + 4)[core]


def along_z(steps):
    return pairs(lambda y, xh, c, z, xl: (y, xh, c, z + steps(y, c), xl))


def to_member(steps):
    def target(y, xh, c, z, xl):
        member = (z - steps(y, c)) % 8
        return (member // 2, xh, member % 2, z, xl)

    return pairs(target)


def own_steps(steps):
    table = [steps(m // 2, m % 2) for m in range(8)]
    member = lax.axis_index(("y", "core"))
    return sum(jnp.where(member == m, d, 0) for m, d in enumerate(table))


def send(x, perm):
    return lax.ppermute(x, AXES, perm)


def rms_normed(rows):
    widened = rows.astype(jnp.float32)
    inv_rms = lax.rsqrt(jnp.mean(widened * widened, axis=-1, keepdims=True) + EPS)
    return (widened * inv_rms).astype(jnp.bfloat16)


def routing(counts, slot_of, slot_count):
    total_rows = slot_of.shape[0]
    numbers = jnp.arange(total_rows, dtype=jnp.int32)
    run_ends = jnp.cumsum(counts)
    starts = run_ends - counts
    sender = jnp.sum((run_ends[None, :] <= numbers[:, None]).astype(jnp.int32), axis=1)
    holder_ids = jnp.arange(counts.shape[0], dtype=jnp.int32)
    own_start = jnp.sum(
        jnp.where(sender[:, None] == holder_ids[None, :], starts[None, :], 0), axis=1
    )
    position = numbers - own_start
    owners = slot_of // slot_count
    within = slot_of % slot_count
    matches = (
        (sender[:, None] == sender[None, :])
        & (owners[:, None] == owners[None, :])
        & (numbers[None, :] < numbers[:, None])
    )
    ordinal = jnp.sum(matches.astype(jnp.int32), axis=1)
    return (sender, position, owners, within, ordinal)


def pack(neighbours, counts, slot_of):
    seq = ("y", "xh", "core")
    seq_count = 16
    own_index = lax.axis_index(seq)
    tok_dev, capacity, feat = neighbours.shape
    pair_cap = -(-capacity // seq_count)
    slot_count = slot_of.shape[0] // seq_count
    columns = seq_count * pair_cap
    sender, position, owners, within, ordinal = routing(counts, slot_of, slot_count)
    send_col = owners * pair_cap + ordinal
    recv_col = sender * pair_cap + ordinal
    column_ids = jnp.arange(columns, dtype=jnp.int32)
    is_mine = sender == own_index
    pick_send = ((column_ids[:, None] == send_col[None, :]) & is_mine[None, :]).astype(jnp.bfloat16)
    pick_local = (jnp.arange(capacity, dtype=jnp.int32)[:, None] == position[None, :]).astype(
        jnp.bfloat16
    )
    select = jnp.dot(pick_send, pick_local.T, preferred_element_type=jnp.float32)
    is_ours = owners == own_index
    pick_slot = (
        (jnp.arange(slot_count, dtype=jnp.int32)[:, None] == within[None, :]) & is_ours[None, :]
    ).astype(jnp.bfloat16)
    pick_recv = (column_ids[:, None] == recv_col[None, :]).astype(jnp.bfloat16)
    placing = jnp.dot(pick_slot, pick_recv.T, preferred_element_type=jnp.float32)
    packed = jnp.einsum(
        "ki,tid->ktd", select.astype(jnp.bfloat16), neighbours, preferred_element_type=jnp.float32
    ).astype(jnp.bfloat16)
    return packed.reshape(columns * tok_dev, feat), placing.astype(jnp.bfloat16)


def place(arrived, placing):
    slot_count, columns = placing.shape
    placed = jnp.einsum(
        "jc,cr->jr", placing, arrived.reshape(columns, -1), preferred_element_type=jnp.float32
    )
    return placed.astype(jnp.bfloat16).reshape(-1, arrived.shape[1])


def matmul(a, b):
    return jnp.dot(a, b, preferred_element_type=jnp.float32)


def matmul_t(a, b):
    return lax.dot_general(a, b, (((1,), (1,)), ((), ())), preferred_element_type=jnp.float32)


def gelu(x):
    return 0.5 * x * (1.0 + lax.erf(x * (2.0**-0.5)))


def encode_kernel(steps, keep_raw, rows, mine, other, result, normed, total):
    step = pl.program_id(0)

    @pl.when(step == 0)
    def _():
        normed[...] = rms_normed(rows[...])
        total[...] = jnp.zeros_like(total)

    for block in (mine, other):
        parts = [block[i] for i in range(block.shape[0])]
        w_in, w_out = jnp.concatenate(parts[0::2], axis=0), jnp.concatenate(parts[1::2], axis=0)
        units = gelu(matmul_t(normed[...], w_in)).astype(jnp.bfloat16)
        total[...] += matmul(units, w_out)

    @pl.when(step == steps - 1)
    def _():
        summed = total[...]
        if keep_raw:
            summed = summed + rows[...].astype(jnp.float32)
        result[...] = summed.astype(result.dtype)


def encode(rows, mine, other, keep_raw):
    count, feat = rows.shape
    planes = 8
    steps = 4
    mine, other = (w.reshape(2 * planes, -1, feat) for w in (mine, other))
    weight = pl.BlockSpec((2 * planes // steps,) + mine.shape[1:], lambda i: (i, 0, 0))
    whole = pl.BlockSpec((count, feat), lambda i: (0, 0))
    return pl.pallas_call(
        lambda *refs: encode_kernel(steps, keep_raw, *refs),
        grid=(steps,),
        in_specs=[whole, weight, weight],
        out_specs=whole,
        out_shape=jax.ShapeDtypeStruct((count, feat), jnp.float32 if keep_raw else jnp.bfloat16),
        scratch_shapes=[
            pltpu.VMEM((count, feat), jnp.bfloat16),
            pltpu.VMEM((count, feat), jnp.float32),
        ],
        compiler_params=pltpu.CompilerParams(vmem_limit_bytes=32 * 2**20),
        cost_estimate=pl.CostEstimate(flops=1, bytes_accessed=1, transcendentals=0),
        name="encode",
    )(rows, mine, other)


def query_kernel(tokens, weight, result):
    projected = matmul(tokens[...], weight[...])
    result[...] = (projected * HD ** (-0.5)).astype(jnp.bfloat16)


def query(tokens, weight):
    return pl.pallas_call(
        query_kernel,
        out_shape=jax.ShapeDtypeStruct((tokens.shape[0], weight.shape[1]), jnp.bfloat16),
        compiler_params=pltpu.CompilerParams(vmem_limit_bytes=40 * 2**20),
        cost_estimate=pl.CostEstimate(flops=1, bytes_accessed=1, transcendentals=0),
        name="query",
    )(tokens, weight)


def attend_kernel(first, q, enc_0, enc_1, kv, mixed):
    feat = kv.shape[0] // 2
    for span, enc in enumerate((enc_0, enc_1)):
        source = enc[...]
        row = first + span * 4 * CT
        keys = matmul(source, kv[:feat]).astype(jnp.bfloat16)
        values = matmul(source, kv[feat:]).astype(jnp.bfloat16)
        for head in range(2):
            columns = slice(head * HD, (head + 1) * HD)
            scores = matmul_t(q[row : row + CT, columns], keys[:, columns])
            exponent = jnp.exp(scores - jnp.max(scores, axis=-1, keepdims=True))
            probs = exponent / jnp.sum(exponent, axis=-1, keepdims=True)
            out = matmul(probs.astype(jnp.bfloat16), values[:, columns])
            mixed[span * CT : (span + 1) * CT, columns] = out.astype(jnp.bfloat16)


def attend(first, q, enc_0, enc_1, kv):
    return pl.pallas_call(
        lambda *refs: attend_kernel(first, *refs),
        out_shape=jax.ShapeDtypeStruct((2 * CT, q.shape[1]), jnp.bfloat16),
        compiler_params=pltpu.CompilerParams(vmem_limit_bytes=32 * 2**20),
        cost_estimate=pl.CostEstimate(flops=1, bytes_accessed=1, transcendentals=0),
        name="attend",
    )(q, enc_0, enc_1, kv)


def project_kernel(mixed_a, mixed_b, weight, near, far):
    half = mixed_a.shape[1]
    width = weight.shape[3]
    for plane in range(weight.shape[0]):
        for block in range(weight.shape[1] // 2):
            start = (plane * weight.shape[1] // 2 + block) * width
            out = matmul(mixed_a[...], weight[plane, block])
            out = out + matmul(mixed_b[...], weight[plane, weight.shape[1] // 2 + block])
            near[:, start : start + width] = out[:CT]
            far[:, start : start + width] = out[CT:].astype(jnp.bfloat16)


def project(mixed_a, mixed_b, weight):
    count, half = mixed_a.shape
    planes, steps = 8, 4
    weight = weight.reshape(planes, -1, half, weight.shape[1])
    blocks = weight.shape[1]
    width = planes * blocks // 2 * weight.shape[3]
    rows = pl.BlockSpec((count, half), lambda i: (0, 0))
    out = pl.BlockSpec((CT, width // steps), lambda i: (0, i))
    return pl.pallas_call(
        project_kernel,
        grid=(steps,),
        in_specs=[
            rows,
            rows,
            pl.BlockSpec((planes // steps,) + weight.shape[1:], lambda i: (i, 0, 0, 0)),
        ],
        out_specs=[out, out],
        out_shape=[
            jax.ShapeDtypeStruct((CT, width), jnp.float32),
            jax.ShapeDtypeStruct((CT, width), jnp.bfloat16),
        ],
        compiler_params=pltpu.CompilerParams(vmem_limit_bytes=32 * 2**20),
        cost_estimate=pl.CostEstimate(flops=1, bytes_accessed=1, transcendentals=0),
        name="project",
    )(mixed_a, mixed_b, weight)


def together(*values):
    return lax.optimization_barrier(values)


def body(
    hidden_states,
    query_weight,
    kv_weight,
    output_weight,
    enc_in_weight,
    enc_out_weight,
    neighbours,
    counts,
    slot_of,
):
    core = lax.axis_index("core")
    plane = lax.axis_index("z")
    feat = neighbours.shape[-1]

    half = enc_in_weight.shape[0] // 2
    sides = [
        lax.dynamic_slice_in_dim(w, core * half, half, 0) for w in (enc_in_weight, enc_out_weight)
    ]
    enc_a = lax.all_gather(jnp.concatenate(sides, axis=0), "z", axis=0, tiled=True)

    def piece_of(weight, steps, axis):
        count = weight.shape[axis] // 8
        index = (plane + own_steps(steps)) % 8
        return lax.dynamic_slice_in_dim(weight, index * count, count, axis)

    width = query_weight.shape[1]
    kv_piece = piece_of(kv_weight, steps_a, 0)
    in_piece = jnp.concatenate(
        [piece_of(query_weight, steps_a, 0), kv_piece[:, 0], kv_piece[:, 1]], axis=0
    )
    out_piece = piece_of(output_weight, steps_b, 1)
    out_piece = jnp.concatenate(
        [out_piece[:, i : i + width] for i in range(0, out_piece.shape[1], width)], axis=0
    )
    normed = rms_normed(hidden_states)

    packed, placing = pack(neighbours, counts, slot_of)
    arrived = lax.all_to_all(packed, ("y", "xh", "core"), split_axis=0, concat_axis=0, tiled=True)
    in_piece = send(in_piece, along_z(steps_a))
    placed = place(arrived, placing)

    placed, in_piece = together(placed, in_piece)
    rows = lax.all_to_all(placed, ("z", "xl"), split_axis=0, concat_axis=0, tiled=True)
    in_piece = send(in_piece, to_member(steps_a))

    rows, in_piece, out_piece, enc_a, normed = together(rows, in_piece, out_piece, enc_a, normed)
    gathered = lax.all_gather(in_piece, "z", axis=0, tiled=True)
    visitors = send(rows, X_OUT)
    enc_b = send(enc_a, CORE)
    out_piece = send(out_piece, along_z(steps_b))
    token_1, token_3 = send(normed, Y_UP[1]), send(normed, Y_UP[3])

    visitors, enc_b, normed = together(visitors, enc_b, normed)
    token_2 = send(normed, Y_UP[2])
    visited = encode(visitors, enc_a, enc_b, keep_raw=False)

    visited, rows, out_piece = together(visited, rows, out_piece)
    returned = send(visited, X_BACK)
    out_piece = send(out_piece, to_member(steps_b))
    encoded = encode(rows, enc_a, enc_b, keep_raw=True)
    encoded = (encoded + returned.astype(jnp.float32)).astype(jnp.bfloat16)

    encoded, normed, token_1, token_2, token_3, out_piece = together(
        encoded, normed, token_1, token_2, token_3, out_piece
    )
    out_pieces = jnp.concatenate([out_piece, send(out_piece, X_OUT)], axis=0)
    out_weight = lax.all_gather(out_pieces, "z", axis=0, tiled=True)
    blocks = [encoded] + [send(encoded, Y_UP[d]) for d in (1, 2, 3)]
    parts = gathered.reshape(8, -1, width)
    q_rows, k_rows = query_weight.shape[0] // 8, feat // 8
    kv_a = jnp.concatenate(
        [
            parts[:, i : i + k_rows].reshape(feat, width)
            for i in (q_rows, q_rows + k_rows)
        ],
        axis=0,
    )
    q_a = parts[:, :q_rows].reshape(-1, width)
    encoded, kv_a, q_a = together(encoded, kv_a, q_a)
    kv_b, q_b = send(kv_a, X_OUT), send(q_a, X_OUT)
    tokens = jnp.concatenate([normed, token_1, token_2, token_3], axis=0)
    tokens = jnp.concatenate([tokens, send(tokens, CORE)], axis=0)
    blocks[0] = encoded
    others = [send(block, CORE) for block in blocks]

    def mix(queries, kv):
        return [attend(d * CT, queries, blocks[d], others[d], kv) for d in range(4)]

    mixed_a = mix(query(tokens, q_a), kv_a)
    mixed_b = mix(query(tokens, q_b), kv_b)

    out_weight, *mixed = together(out_weight, *mixed_a, *mixed_b)
    total = hidden_states.astype(jnp.float32)
    for d in (2, 1, 3, 0):
        near, far = project(mixed[d], mixed[4 + d], out_weight)
        near = near + send(far, CORE).astype(jnp.float32)
        if d:
            near = send(near.astype(jnp.bfloat16), Y_UP[4 - d]).astype(jnp.float32)
        total = total + near
    return total.astype(jnp.bfloat16)


def solution(mesh):
    fine = Mesh(mesh.devices.reshape(SIZES), AXES)
    seq, blk = ("y", "xh", "core"), ("z", "xl")
    placed = (
        P(seq + blk, None),
        P(None, blk),
        P(None, None, blk),
        P(blk, None),
        P(blk, None),
        P(blk, None),
        P(blk, seq, None),
        P(),
        P(),
    )
    return jax.shard_map(
        body, mesh=fine, in_specs=placed, out_specs=P(seq + blk, None), check_vma=False
    )
```

profile of v0, /device:TPU:1, one launch (start us, length us, event | category | flops | bytes accessed | tf_op | source)
XLA Modules:
  0.0 234.3 jit_solution(1683933501028352998)
XLA Ops:
  11.3 1.6 convolution_convert_fusion.1
  13.9 8.4 %all-to-all-start = ((bf16[16,24,896]{2,1,0:T(8,128)(2,1)}), bf16[16,24,896]{2,1,0:T(8,128)(2,1)S(1)}, u32[]{:S(2)}, u32[]{:S(2)}) async-start(bf16[16,24,896]{2,1,0:T(8,128)(2,1)} %bitcast.35), calls=%async_computation | async-start | bytes 1376256 | tf_op jit(solution)/shard_map/all_to_all | solution.py:320
  24.3 8.8 %collective-permute-start = (bf16[736,256]{1,0:T(8,128)(2,1)}, bf16[736,256]{1,0:T(8,128)(2,1)}, u32[]{:S(2)}, u32[]{:S(2)}) collective-permute-start(bf16[736,256]{1,0:T(8,128)(2,1)} %pad_maximum_fusion.4), channel_id=1, source_target_pairs={{0,0},{1,1},{2,2},{3,3},{4,4},{5,5},{6,6},{7,7},{8,8},{9,9},{10,10... | collective-permute-start | bytes 1130504 | tf_op jit(solution)/shard_map/ppermute | solution.py:72
  33.4 2.0 all-to-all-done
  36.6 1.5 convolution_convert_fusion
  39.1 10.1 %collective-permute-done = bf16[736,256]{1,0:T(8,128)(2,1)} collective-permute-done((bf16[736,256]{1,0:T(8,128)(2,1)}, bf16[736,256]{1,0:T(8,128)(2,1)}, u32[]{:S(2)}, u32[]{:S(2)}) %collective-permute-start) | collective-permute-done | bytes 376864 | tf_op jit(solution)/shard_map/ppermute | solution.py:72
  49.2 7.7 %all-to-all-start.1 = ((bf16[16,16,896]{2,1,0:T(8,128)(2,1)}), bf16[16,16,896]{2,1,0:T(8,128)(2,1)S(1)}, u32[]{:S(2)}, u32[]{:S(2)}) async-start(bf16[16,16,896]{2,1,0:T(8,128)(2,1)} %bitcast.5), calls=%async_computation.1 | async-start | bytes 917504 | tf_op jit(solution)/shard_map/all_to_all | solution.py:325
  56.9 4.8 %collective-permute-start.1 = (bf16[736,256]{1,0:T(8,128)(2,1)}, bf16[736,256]{1,0:T(8,128)(2,1)S(1)}, u32[]{:S(2)}, u32[]{:S(2)}) collective-permute-start(bf16[736,256]{1,0:T(8,128)(2,1)} %collective-permute-done), channel_id=1, source_target_pairs={{0,0},{1,1},{2,18},{3,19},{4,68},{5,69},{6,86},{7,87},{8,136},{9,1... | collective-permute-start | bytes 1130504 | tf_op jit(solution)/shard_map/ppermute | solution.py:72
  64.3 2.2 collective-permute-done.1
  66.5 7.6 %all-to-all-done.1 = bf16[16,16,896]{2,1,0:T(8,128)(2,1)S(1)} async-done(((bf16[16,16,896]{2,1,0:T(8,128)(2,1)}), bf16[16,16,896]{2,1,0:T(8,128)(2,1)S(1)}, u32[]{:S(2)}, u32[]{:S(2)}) %all-to-all-start.1) | async-done | bytes 458784 | tf_op jit(solution)/shard_map/all_to_all | solution.py:325
  74.1 2.4 %all-gather.4.cloned.1.call-done = bf16[1792,896]{1,0:T(8,128)(2,1)} async-done(((bf16[224,896]{1,0:T(8,128)(2,1)}), bf16[1792,896]{1,0:T(8,128)(2,1)}) %all-gather.4.cloned.1.call-update) | async-done | bytes 3211280 | tf_op jit(solution)/shard_map/all_gather | solution.py:301
  77.3 2.4 %collective-permute-start.2 = (bf16[256,896]{1,0:T(8,128)(2,1)S(1)}, bf16[256,896]{1,0:T(8,128)(2,1)S(1)}, u32[]{:S(2)}, u32[]{:S(2)}) collective-permute-start(bf16[256,896]{1,0:T(8,128)(2,1)S(1)} %bitcast.31), channel_id=1, source_target_pairs={{0,1},{1,32},{2,3},{3,34},{4,5},{5,36},{6,7},{7,38},{8,9},{9,40},{... | collective-permute-start | bytes 1376264 | tf_op jit(solution)/shard_map/ppermute | solution.py:72
  79.7 4.7 %collective-permute-start.4 = (bf16[512,256]{1,0:T(8,128)(2,1)}, bf16[512,256]{1,0:T(8,128)(2,1)S(1)}, u32[]{:S(2)}, u32[]{:S(2)}) collective-permute-start(bf16[512,256]{1,0:T(8,128)(2,1)} %pad_maximum_fusion.5), channel_id=1, source_target_pairs={{0,0},{1,1},{2,2},{3,3},{4,4},{5,5},{6,6},{7,7},{8,8},{9,9},{10,10... | collective-permute-start | bytes 786440 | tf_op jit(solution)/shard_map/ppermute | solution.py:72
  85.2 1.9 copy-done.3
  87.1 5.0 %encode.2 = bf16[256,896]{1,0:T(8,128)(2,1)S(1)} custom-call(bf16[256,896]{1,0:T(8,128)(2,1)S(1)} %collective-permute-done.2.refs_0_, bf16[16,112,896]{2,1,0:T(8,128)(2,1)S(1)} %bitcast.25, bf16[16,112,896]{2,1,0:T(8,128)(2,1)S(1)} %bitcast.27), custom_call_target="tpu_custom_call" | custom-call | flops 1 | bytes 1 | tf_op jit(solution)/shard_map/encode/pallas_call | solution.py:182
  93.1 8.0 %collective-permute-start.8 = (bf16[64,4096]{1,0:T(8,128)(2,1)S(1)}, bf16[64,4096]{1,0:T(8,128)(2,1)S(1)}, u32[]{:S(2)}, u32[]{:S(2)}) collective-permute-start(bf16[64,4096]{1,0:T(8,128)(2,1)S(1)} %copy-done.5), channel_id=1, source_target_pairs={{0,192},{1,193},{2,194},{3,195},{4,196},{5,197},{6,198},{7,199},{8... | collective-permute-start | bytes 1572872 | tf_op jit(solution)/shard_map/ppermute | solution.py:72
  102.3 5.0 %encode.3 = f32[256,896]{1,0:T(8,128)S(1)} custom-call(bf16[256,896]{1,0:T(8,128)(2,1)S(1)} %bitcast.32, bf16[16,112,896]{2,1,0:T(8,128)(2,1)S(1)} %bitcast.26, bf16[16,112,896]{2,1,0:T(8,128)(2,1)S(1)} %bitcast.28), custom_call_target="tpu_custom_call" | custom-call | flops 1 | bytes 1 | tf_op jit(solution)/shard_map/encode/pallas_call | solution.py:182
  107.3 6.8 %collective-permute-start.9 = (bf16[512,256]{1,0:T(8,128)(2,1)S(1)}, bf16[512,256]{1,0:T(8,128)(2,1)S(1)}, u32[]{:S(2)}, u32[]{:S(2)}) collective-permute-start(bf16[512,256]{1,0:T(8,128)(2,1)S(1)} %collective-permute-done.4), channel_id=1, source_target_pairs={{0,0},{1,1},{2,18},{3,19},{4,68},{5,69},{6,86},{7,87},{8,136},{9,1... | collective-permute-start | bytes 786440 | tf_op jit(solution)/shard_map/ppermute | solution.py:72
  114.2 6.7 %collective-permute-done.8 = bf16[64,4096]{1,0:T(8,128)(2,1)S(1)} collective-permute-done((bf16[64,4096]{1,0:T(8,128)(2,1)S(1)}, bf16[64,4096]{1,0:T(8,128)(2,1)S(1)}, u32[]{:S(2)}, u32[]{:S(2)}) %collective-permute-start.8) | collective-permute-done | bytes 524320 | tf_op jit(solution)/shard_map/ppermute | solution.py:72
  120.9 6.4 %collective-permute-done.9 = bf16[512,256]{1,0:T(8,128)(2,1)S(1)} collective-permute-done((bf16[512,256]{1,0:T(8,128)(2,1)S(1)}, bf16[512,256]{1,0:T(8,128)(2,1)S(1)}, u32[]{:S(2)}, u32[]{:S(2)}) %collective-permute-start.9) | collective-permute-done | bytes 262176 | tf_op jit(solution)/shard_map/ppermute | solution.py:72
  127.3 2.8 %collective-permute-start.10 = (bf16[512,256]{1,0:T(8,128)(2,1)S(1)}, bf16[512,256]{1,0:T(8,128)(2,1)S(1)}, u32[]{:S(2)}, u32[]{:S(2)}) collective-permute-start(bf16[512,256]{1,0:T(8,128)(2,1)S(1)} %collective-permute-done.9), channel_id=1, source_target_pairs={{0,1},{1,32},{2,3},{3,34},{4,5},{5,36},{6,7},{7,38},{8,9},{9,40},{... | collective-permute-start | bytes 786440 | tf_op jit(solution)/shard_map/ppermute | solution.py:72
  130.1 3.3 %collective-permute-done.10 = bf16[512,256]{1,0:T(8,128)(2,1)S(1)} collective-permute-done((bf16[512,256]{1,0:T(8,128)(2,1)S(1)}, bf16[512,256]{1,0:T(8,128)(2,1)S(1)}, u32[]{:S(2)}, u32[]{:S(2)}) %collective-permute-start.10) | collective-permute-done | bytes 262176 | tf_op jit(solution)/shard_map/ppermute | solution.py:72
  134.3 3.1 %pad_maximum_fusion = bf16[256,4096]{1,0:T(8,128)(2,1)} fusion(bf16[64,4096]{1,0:T(8,128)(2,1)} %copy-done.7, bf16[64,4096]{1,0:T(8,128)(2,1)} %copy-done.11, bf16[64,4096]{1,0:T(8,128)(2,1)} %copy-done.9, bf16[64,4096]{1,0:T(8,128)(2,1)} %fusion.2), kind=kLoop, calls=%fused_computation.1 | loop fusion | flops 8388608 | bytes 4194304 | tf_op jit(solution)/shard_map/concatenate | solution.py:363
  138.1 1.8 slice.30
  141.3 2.7 %collective-permute-start.19 = (bf16[4096,256]{1,0:T(8,128)(2,1)S(1)}, bf16[4096,256]{1,0:T(8,128)(2,1)S(1)}, u32[]{:S(2)}, u32[]{:S(2)}) collective-permute-start(bf16[4096,256]{1,0:T(8,128)(2,1)S(1)} %bitcast.29), channel_id=1, source_target_pairs={{0,1},{1,32},{2,3},{3,34},{4,5},{5,36},{6,7},{7,38},{8,9},{9,40},{... | collective-permute-start | bytes 6291464 | tf_op jit(solution)/shard_map/ppermute | solution.py:72
  144.0 1.5 collective-permute-start.13
  145.6 1.8 collective-permute-start.15
  148.2 9.0 %collective-permute-done.13.refs_1_ = bf16[256,896]{1,0:T(8,128)(2,1)S(1)} collective-permute-done((bf16[256,896]{1,0:T(8,128)(2,1)S(1)}, bf16[256,896]{1,0:T(8,128)(2,1)S(1)}, u32[]{:S(2)}, u32[]{:S(2)}) %collective-permute-start.13) | collective-permute-done | bytes 458784 | tf_op jit(solution)/shard_map/ppermute | solution.py:72
  157.2 11.0 %collective-permute-done.15.refs_1_ = bf16[256,896]{1,0:T(8,128)(2,1)S(1)} collective-permute-done((bf16[256,896]{1,0:T(8,128)(2,1)S(1)}, bf16[256,896]{1,0:T(8,128)(2,1)S(1)}, u32[]{:S(2)}, u32[]{:S(2)}) %collective-permute-start.15) | collective-permute-done | bytes 458784 | tf_op jit(solution)/shard_map/ppermute | solution.py:72
  169.7 1.8 constant_dynamic-update-slice_fusion.tokens
  172.8 1.7 attend.8.mixed_a
  174.5 1.7 attend.9.mixed_a
  176.2 1.6 attend.10.mixed_a
  177.9 1.7 attend.11.mixed_a
  180.9 1.6 attend.12.mixed_b
  182.5 1.7 attend.13.mixed_b
  184.2 1.7 attend.14.mixed_b
  185.8 1.7 attend.15.mixed_b
  187.5 2.2 all-gather.6.cloned.1.call-done
  189.7 2.2 copy-done.1
  191.8 1.3 project.6
  194.0 1.3 project.7
  196.1 1.3 project.5
  197.6 1.3 project.4
  201.0 1.5 collective-permute-start.24
  202.6 1.6 collective-permute-start.22
  204.2 10.1 %collective-permute-done.26 = bf16[64,4096]{1,0:T(8,128)(2,1)S(1)} collective-permute-done((bf16[64,4096]{1,0:T(8,128)(2,1)S(1)}, bf16[64,4096]{1,0:T(8,128)(2,1)S(1)}, u32[]{:S(2)}, u32[]{:S(2)}) %collective-permute-start.26) | collective-permute-done | bytes 524320 | tf_op jit(solution)/shard_map/ppermute | solution.py:72
  214.4 12.2 %collective-permute-done.22 = bf16[64,4096]{1,0:T(8,128)(2,1)S(1)} collective-permute-done((bf16[64,4096]{1,0:T(8,128)(2,1)S(1)}, bf16[64,4096]{1,0:T(8,128)(2,1)S(1)}, u32[]{:S(2)}, u32[]{:S(2)}) %collective-permute-start.22) | collective-permute-done | bytes 524320 | tf_op jit(solution)/shard_map/ppermute | solution.py:72
  (109 shorter events, 29.5 us)
Async XLA Ops:
  6.5 17.0 %copy-start = (bf16[4096,256]{1,0:T(8,128)(2,1)S(1)}, bf16[4096,256]{1,0:T(8,128)(2,1)}, u32[]{:S(2)}) copy-start(bf16[4096,256]{1,0:T(8,128)(2,1)} %param.10) | copy-start | bytes 6291460
  6.5 69.9 %all-gather.4.cloned.1.call-start = ((), (), s32[]{:S(2)}) async-start(), calls=%async_computation.2 | async-start | bytes 3612672 | tf_op jit(solution)/shard_map/all_gather | solution.py:301
  6.5 26.6 %copy-start.4 = (bf16[64,4096]{1,0:T(8,128)(2,1)S(1)}, bf16[64,4096]{1,0:T(8,128)(2,1)}, u32[]{:S(2)}) copy-start(bf16[64,4096]{1,0:T(8,128)(2,1)} %param.9) | copy-start | bytes 1572868
  7.8 25.6 %copy-start.14 = (s32[512]{0:T(512)S(1)}, s32[512]{0:T(512)}, u32[]{:S(2)}) copy-start(s32[512]{0:T(512)} %param.17) | copy-start | bytes 6148
  13.9 21.5 %all-to-all-start = ((bf16[16,24,896]{2,1,0:T(8,128)(2,1)}), bf16[16,24,896]{2,1,0:T(8,128)(2,1)S(1)}, u32[]{:S(2)}, u32[]{:S(2)}) async-start(bf16[16,24,896]{2,1,0:T(8,128)(2,1)} %bitcast.35), calls=%async_computation | async-start | bytes 1376256 | tf_op jit(solution)/shard_map/all_to_all | solution.py:320
  24.3 24.9 %collective-permute-start = (bf16[736,256]{1,0:T(8,128)(2,1)}, bf16[736,256]{1,0:T(8,128)(2,1)}, u32[]{:S(2)}, u32[]{:S(2)}) collective-permute-start(bf16[736,256]{1,0:T(8,128)(2,1)} %pad_maximum_fusion.4), channel_id=1, source_target_pairs={{0,0},{1,1},{2,2},{3,3},{4,4},{5,5},{6,6},{7,7},{8,8},{9,9},{10,10... | collective-permute-start | bytes 1130504 | tf_op jit(solution)/shard_map/ppermute | solution.py:72
  49.2 24.9 %all-to-all-start.1 = ((bf16[16,16,896]{2,1,0:T(8,128)(2,1)}), bf16[16,16,896]{2,1,0:T(8,128)(2,1)S(1)}, u32[]{:S(2)}, u32[]{:S(2)}) async-start(bf16[16,16,896]{2,1,0:T(8,128)(2,1)} %bitcast.5), calls=%async_computation.1 | async-start | bytes 917504 | tf_op jit(solution)/shard_map/all_to_all | solution.py:325
  56.9 81.2 %all-gather.8.cloned.1.call-start = ((), (), s32[]{:S(2)}) async-start(), calls=%async_computation.4 | async-start | bytes 3391488 | tf_op jit(solution)/shard_map/all_gather | solution.py:329
  56.9 9.6 %collective-permute-start.1 = (bf16[736,256]{1,0:T(8,128)(2,1)}, bf16[736,256]{1,0:T(8,128)(2,1)S(1)}, u32[]{:S(2)}, u32[]{:S(2)}) collective-permute-start(bf16[736,256]{1,0:T(8,128)(2,1)} %collective-permute-done), channel_id=1, source_target_pairs={{0,0},{1,1},{2,18},{3,19},{4,68},{5,69},{6,86},{7,87},{8,136},{9,1... | collective-permute-start | bytes 1130504 | tf_op jit(solution)/shard_map/ppermute | solution.py:72
  66.5 10.0 %copy-start.13 = (bf16[736,256]{1,0:T(8,128)(2,1)}, bf16[736,256]{1,0:T(8,128)(2,1)S(1)}, u32[]{:S(2)}) copy-start(bf16[736,256]{1,0:T(8,128)(2,1)S(1)} %collective-permute-done.1) | copy-start | bytes 1130500
  76.5 113.1 %all-gather.6.cloned.1.call-start = ((), (), s32[]{:S(2)}) async-start(), calls=%async_computation.3 | async-start | bytes 4718592 | tf_op jit(solution)/shard_map/all_gather | solution.py:349
  76.5 8.6 %collective-permute-start.3 = (bf16[1792,896]{1,0:T(8,128)(2,1)}, bf16[1792,896]{1,0:T(8,128)(2,1)S(1)}, u32[]{:S(2)}, u32[]{:S(2)}) collective-permute-start(bf16[1792,896]{1,0:T(8,128)(2,1)} %all-gather.4.cloned.1.call-done), channel_id=1, source_target_pairs={{0,16},{1,17},{2,18},{3,19},{4,20},{5,21},{6,22},{7,23},{8,24},{9,... | collective-permute-start | bytes 9633800 | tf_op jit(solution)/shard_map/ppermute | solution.py:72
  77.3 7.8 %collective-permute-start.2 = (bf16[256,896]{1,0:T(8,128)(2,1)S(1)}, bf16[256,896]{1,0:T(8,128)(2,1)S(1)}, u32[]{:S(2)}, u32[]{:S(2)}) collective-permute-start(bf16[256,896]{1,0:T(8,128)(2,1)S(1)} %bitcast.31), channel_id=1, source_target_pairs={{0,1},{1,32},{2,3},{3,34},{4,5},{5,36},{6,7},{7,38},{8,9},{9,40},{... | collective-permute-start | bytes 1376264 | tf_op jit(solution)/shard_map/ppermute | solution.py:72
  79.7 12.3 %collective-permute-start.4 = (bf16[512,256]{1,0:T(8,128)(2,1)}, bf16[512,256]{1,0:T(8,128)(2,1)S(1)}, u32[]{:S(2)}, u32[]{:S(2)}) collective-permute-start(bf16[512,256]{1,0:T(8,128)(2,1)} %pad_maximum_fusion.5), channel_id=1, source_target_pairs={{0,0},{1,1},{2,2},{3,3},{4,4},{5,5},{6,6},{7,7},{8,8},{9,9},{10,10... | collective-permute-start | bytes 786440 | tf_op jit(solution)/shard_map/ppermute | solution.py:72
  85.2 1.9 copy-start.3
  87.1 6.0 %copy-start.5 = (bf16[64,4096]{1,0:T(8,128)(2,1)S(1)}, bf16[64,4096]{1,0:T(8,128)(2,1)}, u32[]{:S(2)}) copy-start(bf16[64,4096]{1,0:T(8,128)(2,1)} %fusion.2) | copy-start | bytes 1572868
  92.1 22.0 %collective-permute-start.5 = (bf16[256,896]{1,0:T(8,128)(2,1)S(1)}, bf16[256,896]{1,0:T(8,128)(2,1)S(1)}, u32[]{:S(2)}, u32[]{:S(2)}) collective-permute-start(bf16[256,896]{1,0:T(8,128)(2,1)S(1)} %encode.2), channel_id=1, source_target_pairs={{0,33},{1,0},{2,35},{3,2},{4,37},{5,4},{6,39},{7,6},{8,41},{9,8},{... | collective-permute-start | bytes 1376264 | tf_op jit(solution)/shard_map/ppermute | solution.py:72
  93.1 21.1 %collective-permute-start.6 = (bf16[64,4096]{1,0:T(8,128)(2,1)S(1)}, bf16[64,4096]{1,0:T(8,128)(2,1)S(1)}, u32[]{:S(2)}, u32[]{:S(2)}) collective-permute-start(bf16[64,4096]{1,0:T(8,128)(2,1)S(1)} %copy-done.5), channel_id=1, source_target_pairs={{0,64},{1,65},{2,66},{3,67},{4,68},{5,69},{6,70},{7,71},{8,72},{9,... | collective-permute-start | bytes 1572872 | tf_op jit(solution)/shard_map/ppermute | solution.py:72
  93.1 27.8 %collective-permute-start.8 = (bf16[64,4096]{1,0:T(8,128)(2,1)S(1)}, bf16[64,4096]{1,0:T(8,128)(2,1)S(1)}, u32[]{:S(2)}, u32[]{:S(2)}) collective-permute-start(bf16[64,4096]{1,0:T(8,128)(2,1)S(1)} %copy-done.5), channel_id=1, source_target_pairs={{0,192},{1,193},{2,194},{3,195},{4,196},{5,197},{6,198},{7,199},{8... | collective-permute-start | bytes 1572872 | tf_op jit(solution)/shard_map/ppermute | solution.py:72
  101.1 26.2 %collective-permute-start.7 = (bf16[64,4096]{1,0:T(8,128)(2,1)S(1)}, bf16[64,4096]{1,0:T(8,128)(2,1)S(1)}, u32[]{:S(2)}, u32[]{:S(2)}) collective-permute-start(bf16[64,4096]{1,0:T(8,128)(2,1)S(1)} %copy-done.5), channel_id=1, source_target_pairs={{0,128},{1,129},{2,130},{3,131},{4,132},{5,133},{6,134},{7,135},{8... | collective-permute-start | bytes 1572872 | tf_op jit(solution)/shard_map/ppermute | solution.py:72
  107.3 20.0 %collective-permute-start.9 = (bf16[512,256]{1,0:T(8,128)(2,1)S(1)}, bf16[512,256]{1,0:T(8,128)(2,1)S(1)}, u32[]{:S(2)}, u32[]{:S(2)}) collective-permute-start(bf16[512,256]{1,0:T(8,128)(2,1)S(1)} %collective-permute-done.4), channel_id=1, source_target_pairs={{0,0},{1,1},{2,18},{3,19},{4,68},{5,69},{6,86},{7,87},{8,136},{9,1... | collective-permute-start | bytes 786440 | tf_op jit(solution)/shard_map/ppermute | solution.py:72
  114.2 15.9 %copy-start.9 = (bf16[64,4096]{1,0:T(8,128)(2,1)}, bf16[64,4096]{1,0:T(8,128)(2,1)S(1)}, u32[]{:S(2)}) copy-start(bf16[64,4096]{1,0:T(8,128)(2,1)S(1)} %collective-permute-done.6) | copy-start | bytes 1572868
  120.9 6.4 %copy-start.7 = (bf16[64,4096]{1,0:T(8,128)(2,1)}, bf16[64,4096]{1,0:T(8,128)(2,1)S(1)}, u32[]{:S(2)}) copy-start(bf16[64,4096]{1,0:T(8,128)(2,1)S(1)} %collective-permute-done.8) | copy-start | bytes 1572868
  127.3 6.1 %copy-start.11 = (bf16[64,4096]{1,0:T(8,128)(2,1)}, bf16[64,4096]{1,0:T(8,128)(2,1)S(1)}, u32[]{:S(2)}) copy-start(bf16[64,4096]{1,0:T(8,128)(2,1)S(1)} %collective-permute-done.7) | copy-start | bytes 1572868
  127.3 6.1 %collective-permute-start.10 = (bf16[512,256]{1,0:T(8,128)(2,1)S(1)}, bf16[512,256]{1,0:T(8,128)(2,1)S(1)}, u32[]{:S(2)}, u32[]{:S(2)}) collective-permute-start(bf16[512,256]{1,0:T(8,128)(2,1)S(1)} %collective-permute-done.9), channel_id=1, source_target_pairs={{0,1},{1,32},{2,3},{3,34},{4,5},{5,36},{6,7},{7,38},{8,9},{9,40},{... | collective-permute-start | bytes 786440 | tf_op jit(solution)/shard_map/ppermute | solution.py:72
  137.4 32.3 %collective-permute-start.11 = (bf16[256,4096]{1,0:T(8,128)(2,1)}, bf16[256,4096]{1,0:T(8,128)(2,1)}, u32[]{:S(2)}, u32[]{:S(2)}) collective-permute-start(bf16[256,4096]{1,0:T(8,128)(2,1)} %pad_maximum_fusion), channel_id=1, source_target_pairs={{0,16},{1,17},{2,18},{3,19},{4,20},{5,21},{6,22},{7,23},{8,24},{9,... | collective-permute-start | bytes 6291464 | tf_op jit(solution)/shard_map/ppermute | solution.py:72
  138.0 6.0 %copy-start.6 = (bf16[64,4096]{1,0:T(8,128)(2,1)S(1)}, bf16[64,4096]{1,0:T(8,128)(2,1)}, u32[]{:S(2)}) copy-start(bf16[64,4096]{1,0:T(8,128)(2,1)} %fusion.2) | copy-start | bytes 1572868
  138.0 10.0 %copy-start.10 = (bf16[64,4096]{1,0:T(8,128)(2,1)S(1)}, bf16[64,4096]{1,0:T(8,128)(2,1)}, u32[]{:S(2)}) copy-start(bf16[64,4096]{1,0:T(8,128)(2,1)} %copy-done.9) | copy-start | bytes 1572868
  138.0 10.1 %copy-start.12 = (bf16[64,4096]{1,0:T(8,128)(2,1)S(1)}, bf16[64,4096]{1,0:T(8,128)(2,1)}, u32[]{:S(2)}) copy-start(bf16[64,4096]{1,0:T(8,128)(2,1)} %copy-done.11) | copy-start | bytes 1572868
  139.9 29.1 %copy-start.8 = (bf16[64,4096]{1,0:T(8,128)(2,1)S(1)}, bf16[64,4096]{1,0:T(8,128)(2,1)}, u32[]{:S(2)}) copy-start(bf16[64,4096]{1,0:T(8,128)(2,1)} %copy-done.7) | copy-start | bytes 1572868
  141.3 38.2 %collective-permute-start.19 = (bf16[4096,256]{1,0:T(8,128)(2,1)S(1)}, bf16[4096,256]{1,0:T(8,128)(2,1)S(1)}, u32[]{:S(2)}, u32[]{:S(2)}) collective-permute-start(bf16[4096,256]{1,0:T(8,128)(2,1)S(1)} %bitcast.29), channel_id=1, source_target_pairs={{0,1},{1,32},{2,3},{3,34},{4,5},{5,36},{6,7},{7,38},{8,9},{9,40},{... | collective-permute-start | bytes 6291464 | tf_op jit(solution)/shard_map/ppermute | solution.py:72
  144.0 13.1 %collective-permute-start.13 = (bf16[256,896]{1,0:T(8,128)(2,1)S(1)}, bf16[256,896]{1,0:T(8,128)(2,1)S(1)}, u32[]{:S(2)}, u32[]{:S(2)}) collective-permute-start(bf16[256,896]{1,0:T(8,128)(2,1)S(1)} %add_convert_fusion.3.refs_1_), channel_id=1, source_target_pairs={{0,64},{1,65},{2,66},{3,67},{4,68},{5,69},{6,70},{7,71},{8,72},{9,... | collective-permute-start | bytes 1376264 | tf_op jit(solution)/shard_map/ppermute | solution.py:72
  145.6 22.6 %collective-permute-start.15 = (bf16[256,896]{1,0:T(8,128)(2,1)S(1)}, bf16[256,896]{1,0:T(8,128)(2,1)S(1)}, u32[]{:S(2)}, u32[]{:S(2)}) collective-permute-start(bf16[256,896]{1,0:T(8,128)(2,1)S(1)} %add_convert_fusion.3.refs_1_), channel_id=1, source_target_pairs={{0,128},{1,129},{2,130},{3,131},{4,132},{5,133},{6,134},{7,135},{8... | collective-permute-start | bytes 1376264 | tf_op jit(solution)/shard_map/ppermute | solution.py:72
  147.4 21.6 %collective-permute-start.17 = (bf16[256,896]{1,0:T(8,128)(2,1)S(1)}, bf16[256,896]{1,0:T(8,128)(2,1)S(1)}, u32[]{:S(2)}, u32[]{:S(2)}) collective-permute-start(bf16[256,896]{1,0:T(8,128)(2,1)S(1)} %add_convert_fusion.3.refs_1_), channel_id=1, source_target_pairs={{0,192},{1,193},{2,194},{3,195},{4,196},{5,197},{6,198},{7,199},{8... | collective-permute-start | bytes 1376264 | tf_op jit(solution)/shard_map/ppermute | solution.py:72
  157.2 11.9 %collective-permute-start.12 = (bf16[256,896]{1,0:T(8,128)(2,1)S(1)}, bf16[256,896]{1,0:T(8,128)(2,1)S(1)}, u32[]{:S(2)}, u32[]{:S(2)}) collective-permute-start(bf16[256,896]{1,0:T(8,128)(2,1)S(1)} %add_convert_fusion.3.refs_1_), channel_id=1, source_target_pairs={{0,16},{1,17},{2,18},{3,19},{4,20},{5,21},{6,22},{7,23},{8,24},{9,... | collective-permute-start | bytes 1376264 | tf_op jit(solution)/shard_map/ppermute | solution.py:72
  168.2 12.6 %collective-permute-start.20 = (bf16[1792,256]{1,0:T(8,128)(2,1)S(1)}, bf16[1792,256]{1,0:T(8,128)(2,1)S(1)}, u32[]{:S(2)}, u32[]{:S(2)}) collective-permute-start(bf16[1792,256]{1,0:T(8,128)(2,1)S(1)} %pad_maximum_fusion.1.refs_3_), channel_id=1, source_target_pairs={{0,1},{1,32},{2,3},{3,34},{4,5},{5,36},{6,7},{7,38},{8,9},{9,40},{... | collective-permute-start | bytes 2752520 | tf_op jit(solution)/shard_map/ppermute | solution.py:72
  169.0 5.5 %collective-permute-start.14 = (bf16[256,896]{1,0:T(8,128)(2,1)S(1)}, bf16[256,896]{1,0:T(8,128)(2,1)S(1)}, u32[]{:S(2)}, u32[]{:S(2)}) collective-permute-start(bf16[256,896]{1,0:T(8,128)(2,1)S(1)} %collective-permute-done.13.refs_1_), channel_id=1, source_target_pairs={{0,16},{1,17},{2,18},{3,19},{4,20},{5,21},{6,22},{7,23},{8,24},{9,... | collective-permute-start | bytes 1376264 | tf_op jit(solution)/shard_map/ppermute | solution.py:72
  169.1 7.0 %collective-permute-start.16 = (bf16[256,896]{1,0:T(8,128)(2,1)S(1)}, bf16[256,896]{1,0:T(8,128)(2,1)S(1)}, u32[]{:S(2)}, u32[]{:S(2)}) collective-permute-start(bf16[256,896]{1,0:T(8,128)(2,1)S(1)} %collective-permute-done.15.refs_1_), channel_id=1, source_target_pairs={{0,16},{1,17},{2,18},{3,19},{4,20},{5,21},{6,22},{7,23},{8,24},{9,... | collective-permute-start | bytes 1376264 | tf_op jit(solution)/shard_map/ppermute | solution.py:72
  169.6 8.2 %collective-permute-start.18 = (bf16[256,896]{1,0:T(8,128)(2,1)S(1)}, bf16[256,896]{1,0:T(8,128)(2,1)S(1)}, u32[]{:S(2)}, u32[]{:S(2)}) collective-permute-start(bf16[256,896]{1,0:T(8,128)(2,1)S(1)} %collective-permute-done.17.refs_1_), channel_id=1, source_target_pairs={{0,16},{1,17},{2,18},{3,19},{4,20},{5,21},{6,22},{7,23},{8,24},{9,... | collective-permute-start | bytes 1376264 | tf_op jit(solution)/shard_map/ppermute | solution.py:72
  189.7 2.2 copy-start.1
  191.8 2.2 copy-start.2
  193.2 6.3 %collective-permute-start.25 = (bf16[64,4096]{1,0:T(8,128)(2,1)S(1)}, bf16[64,4096]{1,0:T(8,128)(2,1)S(1)}, u32[]{:S(2)}, u32[]{:S(2)}) collective-permute-start(bf16[64,4096]{1,0:T(8,128)(2,1)S(1)} %get-tuple-element.78), channel_id=1, source_target_pairs={{0,16},{1,17},{2,18},{3,19},{4,20},{5,21},{6,22},{7,23},{8,24},{9,... | collective-permute-start | bytes 1572872 | tf_op jit(solution)/shard_map/ppermute | solution.py:72
  195.4 8.9 %collective-permute-start.27 = (bf16[64,4096]{1,0:T(8,128)(2,1)S(1)}, bf16[64,4096]{1,0:T(8,128)(2,1)S(1)}, u32[]{:S(2)}, u32[]{:S(2)}) collective-permute-start(bf16[64,4096]{1,0:T(8,128)(2,1)S(1)} %get-tuple-element.82), channel_id=1, source_target_pairs={{0,16},{1,17},{2,18},{3,19},{4,20},{5,21},{6,22},{7,23},{8,24},{9,... | collective-permute-start | bytes 1572872 | tf_op jit(solution)/shard_map/ppermute | solution.py:72
  197.5 3.4 %collective-permute-start.23 = (bf16[64,4096]{1,0:T(8,128)(2,1)S(1)}, bf16[64,4096]{1,0:T(8,128)(2,1)S(1)}, u32[]{:S(2)}, u32[]{:S(2)}) collective-permute-start(bf16[64,4096]{1,0:T(8,128)(2,1)S(1)} %get-tuple-element.74), channel_id=1, source_target_pairs={{0,16},{1,17},{2,18},{3,19},{4,20},{5,21},{6,22},{7,23},{8,24},{9,... | collective-permute-start | bytes 1572872 | tf_op jit(solution)/shard_map/ppermute | solution.py:72
  198.9 3.6 %collective-permute-start.21 = (bf16[64,4096]{1,0:T(8,128)(2,1)S(1)}, bf16[64,4096]{1,0:T(8,128)(2,1)S(1)}, u32[]{:S(2)}, u32[]{:S(2)}) collective-permute-start(bf16[64,4096]{1,0:T(8,128)(2,1)S(1)} %get-tuple-element.70), channel_id=1, source_target_pairs={{0,16},{1,17},{2,18},{3,19},{4,20},{5,21},{6,22},{7,23},{8,24},{9,... | collective-permute-start | bytes 1572872 | tf_op jit(solution)/shard_map/ppermute | solution.py:72
  199.6 14.8 %collective-permute-start.26 = (bf16[64,4096]{1,0:T(8,128)(2,1)S(1)}, bf16[64,4096]{1,0:T(8,128)(2,1)S(1)}, u32[]{:S(2)}, u32[]{:S(2)}) collective-permute-start(bf16[64,4096]{1,0:T(8,128)(2,1)S(1)} %add_convert_fusion), channel_id=1, source_target_pairs={{0,64},{1,65},{2,66},{3,67},{4,68},{5,69},{6,70},{7,71},{8,72},{9,... | collective-permute-start | bytes 1572872 | tf_op jit(solution)/shard_map/ppermute | solution.py:72
  201.0 13.4 %collective-permute-start.24 = (bf16[64,4096]{1,0:T(8,128)(2,1)S(1)}, bf16[64,4096]{1,0:T(8,128)(2,1)S(1)}, u32[]{:S(2)}, u32[]{:S(2)}) collective-permute-start(bf16[64,4096]{1,0:T(8,128)(2,1)S(1)} %add_convert_fusion.1), channel_id=1, source_target_pairs={{0,192},{1,193},{2,194},{3,195},{4,196},{5,197},{6,198},{7,199},{8... | collective-permute-start | bytes 1572872 | tf_op jit(solution)/shard_map/ppermute | solution.py:72
  202.6 24.0 %collective-permute-start.22 = (bf16[64,4096]{1,0:T(8,128)(2,1)S(1)}, bf16[64,4096]{1,0:T(8,128)(2,1)S(1)}, u32[]{:S(2)}, u32[]{:S(2)}) collective-permute-start(bf16[64,4096]{1,0:T(8,128)(2,1)S(1)} %add_convert_fusion.2), channel_id=1, source_target_pairs={{0,128},{1,129},{2,130},{3,131},{4,132},{5,133},{6,134},{7,135},{8... | collective-permute-start | bytes 1572872 | tf_op jit(solution)/shard_map/ppermute | solution.py:72
Sparse Core Ops, SparseCore 0:
  9.1 67.2 all-gather.3
  78.3 45.3 all-gather.7
  134.4 55.2 all-gather.5
where the time goes:
time: 235 us; the launch traced here: 234 us
  waiting for transfers between devices  86.1 us (37%)
  starting transfers between devices  72.9 us (31%)
  Pallas kernels  31 us (13%)
  local copies, waits for them, and re-layouts  16.6 us (7%)
  between operations  13.6 us (6%)
  other arithmetic  11 us (5%)
  matrix products  3.08 us (1%)
    ppermute x28, waiting for transfers between devices, send(): return lax.ppermute(x, AXES, perm)  72 us
    ppermute x28, starting transfers between devices, send(): return lax.ppermute(x, AXES, perm)  56.7 us
    pallas_call x8, Pallas kernels, attend(): pl.pallas_call(lambda *refs: attend_kernel(first, *refs), out_shape=jax.S...  13.2 us
    pallas_call x2, Pallas kernels, encode(): pl.pallas_call(lambda *refs: encode_kernel(steps, keep_raw, *refs), grid=...  10 us
    all_to_all x1, starting transfers between devices, body(): lax.all_to_all(packed, ('y', 'xh', 'core'), split_axis=0, concat_axis=0,...  8.45 us
    all_to_all x1, starting transfers between devices, body(): lax.all_to_all(placed, ('z', 'xl'), split_axis=0, concat_axis=0, tiled=True)  7.66 us
    all_to_all x1, waiting for transfers between devices, body(): lax.all_to_all(placed, ('z', 'xl'), split_axis=0, concat_axis=0, tiled=True)  7.57 us
    pallas_call x4, Pallas kernels, project(): pl.pallas_call(project_kernel, grid=(steps,), in_specs=[rows, rows, pl.Bl...  5.31 us
  transfers between devices with their start and end apart: 33, of which 15 were waited for; matrix products, arithmetic and copies ran while one was open for 10% of the time, Pallas kernels for 13%

commit v1 on v0

--- a/solution.py
+++ b/solution.py
@@ -319,9 +319,10 @@
     packed, placing = pack(neighbours, counts, slot_of)
     arrived = lax.all_to_all(packed, ("y", "xh", "core"), split_axis=0, concat_axis=0, tiled=True)
     in_piece = send(in_piece, along_z(steps_a))
+    token_1, token_3 = send(normed, Y_UP[1]), send(normed, Y_UP[3])
     placed = place(arrived, placing)
 
-    placed, in_piece = together(placed, in_piece)
+    placed, in_piece, token_1, token_3 = together(placed, in_piece, token_1, token_3)
     rows = lax.all_to_all(placed, ("z", "xl"), split_axis=0, concat_axis=0, tiled=True)
     in_piece = send(in_piece, to_member(steps_a))
 
@@ -330,22 +331,21 @@
     visitors = send(rows, X_OUT)
     enc_b = send(enc_a, CORE)
     out_piece = send(out_piece, along_z(steps_b))
-    token_1, token_3 = send(normed, Y_UP[1]), send(normed, Y_UP[3])
-
-    visitors, enc_b, normed = together(visitors, enc_b, normed)
     token_2 = send(normed, Y_UP[2])
+
+    visitors, enc_b, out_piece = together(visitors, enc_b, out_piece)
+    out_piece = send(out_piece, to_member(steps_b))
     visited = encode(visitors, enc_a, enc_b, keep_raw=False)
 
     visited, rows, out_piece = together(visited, rows, out_piece)
     returned = send(visited, X_BACK)
-    out_piece = send(out_piece, to_member(steps_b))
+    out_pieces = jnp.concatenate([out_piece, send(out_piece, X_OUT)], axis=0)
     encoded = encode(rows, enc_a, enc_b, keep_raw=True)
     encoded = (encoded + returned.astype(jnp.float32)).astype(jnp.bfloat16)
 
-    encoded, normed, token_1, token_2, token_3, out_piece = together(
-        encoded, normed, token_1, token_2, token_3, out_piece
-    )
-    out_pieces = jnp.concatenate([out_piece, send(out_piece, X_OUT)], axis=0)
+    encoded, normed, token_1, token_2, token_3, out_pieces, gathered = together(
+        encoded, normed, token_1, token_2, token_3, out_pieces, gathered
+    )
     out_weight = lax.all_gather(out_pieces, "z", axis=0, tiled=True)
     blocks = [encoded] + [send(encoded, Y_UP[d]) for d in (1, 2, 3)]
     parts = gathered.reshape(8, -1, width)
@@ -358,17 +358,16 @@
         axis=0,
     )
     q_a = parts[:, :q_rows].reshape(-1, width)
-    encoded, kv_a, q_a = together(encoded, kv_a, q_a)
     kv_b, q_b = send(kv_a, X_OUT), send(q_a, X_OUT)
     tokens = jnp.concatenate([normed, token_1, token_2, token_3], axis=0)
     tokens = jnp.concatenate([tokens, send(tokens, CORE)], axis=0)
-    blocks[0] = encoded
     others = [send(block, CORE) for block in blocks]
 
     def mix(queries, kv):
         return [attend(d * CT, queries, blocks[d], others[d], kv) for d in range(4)]
 
     mixed_a = mix(query(tokens, q_a), kv_a)
+    q_b, *mixed_a = together(q_b, *mixed_a)
     mixed_b = mix(query(tokens, q_b), kv_b)
 
     out_weight, *mixed = together(out_weight, *mixed_a, *mixed_b)

time: 235 us -> 224 us (0.953)
  waiting for transfers between devices: 86.1 us -> 78.8 us
  starting transfers between devices: 72.9 us -> 69.5 us
    ppermute x28, waiting for transfers between devices: 72 us -> 61.2 us  [send(): return lax.ppermute(x, AXES, perm)]
    unnamed x34 -> x20, local copies, waits for them, and re-layouts: 4.37 us -> 8.5 us
    all_gather x1, waiting for transfers between devices: 2.16 us -> 5.46 us  [body(): out_weight = lax.all_gather(out_pieces, 'z', axis=0, tiled=True)]
    all_gather x1, waiting for transfers between devices: 0.01 us -> 2.81 us  [body(): gathered = lax.all_gather(in_piece, 'z', axis=0, tiled=True)]
    all_gather x1, waiting for transfers between devices: 2.39 us -> 0.01 us  [body(): lax.all_gather(jnp.concatenate(sides, axis=0), 'z', axis=0, tiled=True)]
  transfers between devices with their start and end apart: 33 -> 33, of which waited for: 15 -> 15; matrix products, arithmetic and copies ran while one was open for 10% -> 10% of each run, Pallas kernels for 13% -> 14%
where the time goes in v1:
time: 224 us; the launch traced here: 223 us
  waiting for transfers between devices  78.8 us (35%)
  starting transfers between devices  69.5 us (31%)
  Pallas kernels  31.8 us (14%)
  local copies, waits for them, and re-layouts  15.3 us (7%)
  between operations  13.6 us (6%)
  other arithmetic  12.2 us (5%)
    ppermute x28, waiting for transfers between devices, send(): return lax.ppermute(x, AXES, perm)  61.2 us
    ppermute x28, starting transfers between devices, send(): return lax.ppermute(x, AXES, perm)  55.3 us
    pallas_call x8, Pallas kernels, attend(): pl.pallas_call(lambda *refs: attend_kernel(first, *refs), out_shape=jax.S...  13.2 us
    pallas_call x2, Pallas kernels, encode(): pl.pallas_call(lambda *refs: encode_kernel(steps, keep_raw, *refs), grid=...  10.8 us
    unnamed x20, local copies, waits for them, and re-layouts  8.5 us
    all_to_all x1, starting transfers between devices, body(): lax.all_to_all(placed, ('z', 'xl'), split_axis=0, concat_axis=0, tiled=True)  7.2 us
    all_to_all x1, waiting for transfers between devices, body(): lax.all_to_all(placed, ('z', 'xl'), split_axis=0, concat_axis=0, tiled=True)  7.08 us
    all_to_all x1, starting transfers between devices, body(): lax.all_to_all(packed, ('y', 'xh', 'core'), split_axis=0, concat_axis=0,...  6.91 us
  transfers between devices with their start and end apart: 33, of which 15 were waited for; matrix products, arithmetic and copies ran while one was open for 10% of the time, Pallas kernels for 14%

profile of v1, /device:TPU:1, one launch (start us, length us, event | category | flops | bytes accessed | tf_op | source)
XLA Modules:
  0.0 223.2 jit_solution(2660749052260700360)
XLA Ops:
  9.8 2.0 fusion.2
  11.8 2.1 collective-permute-start.1
  13.9 1.4 collective-permute-start.2
  18.1 1.6 convolution_convert_fusion.1
  20.7 6.9 %all-to-all-start = ((bf16[16,24,896]{2,1,0:T(8,128)(2,1)}), bf16[16,24,896]{2,1,0:T(8,128)(2,1)S(1)}, u32[]{:S(2)}, u32[]{:S(2)}) async-start(bf16[16,24,896]{2,1,0:T(8,128)(2,1)} %bitcast.2), calls=%async_computation | async-start | bytes 1376256 | tf_op jit(solution)/shard_map/all_to_all | solution.py:320
  29.6 8.8 %collective-permute-start = (bf16[736,256]{1,0:T(8,128)(2,1)}, bf16[736,256]{1,0:T(8,128)(2,1)}, u32[]{:S(2)}, u32[]{:S(2)}) collective-permute-start(bf16[736,256]{1,0:T(8,128)(2,1)} %pad_maximum_fusion.4), channel_id=1, source_target_pairs={{0,0},{1,1},{2,2},{3,3},{4,4},{5,5},{6,6},{7,7},{8,8},{9,9},{10,10... | collective-permute-start | bytes 1130504 | tf_op jit(solution)/shard_map/ppermute | solution.py:72
  38.4 2.2 all-to-all-done
  42.4 13.1 %collective-permute-done = bf16[736,256]{1,0:T(8,128)(2,1)} collective-permute-done((bf16[736,256]{1,0:T(8,128)(2,1)}, bf16[736,256]{1,0:T(8,128)(2,1)}, u32[]{:S(2)}, u32[]{:S(2)}) %collective-permute-start) | collective-permute-done | bytes 376864 | tf_op jit(solution)/shard_map/ppermute | solution.py:72
  55.5 7.2 %all-to-all-start.1 = ((bf16[16,16,896]{2,1,0:T(8,128)(2,1)}), bf16[16,16,896]{2,1,0:T(8,128)(2,1)S(1)}, u32[]{:S(2)}, u32[]{:S(2)}) async-start(bf16[16,16,896]{2,1,0:T(8,128)(2,1)} %bitcast.5), calls=%async_computation.1 | async-start | bytes 917504 | tf_op jit(solution)/shard_map/all_to_all | solution.py:326
  62.7 3.9 %collective-permute-start.3 = (bf16[736,256]{1,0:T(8,128)(2,1)}, bf16[736,256]{1,0:T(8,128)(2,1)S(1)}, u32[]{:S(2)}, u32[]{:S(2)}) collective-permute-start(bf16[736,256]{1,0:T(8,128)(2,1)} %collective-permute-done), channel_id=1, source_target_pairs={{0,0},{1,1},{2,18},{3,19},{4,68},{5,69},{6,86},{7,87},{8,136},{9,1... | collective-permute-start | bytes 1130504 | tf_op jit(solution)/shard_map/ppermute | solution.py:72
  67.8 3.9 %collective-permute-done.3 = bf16[736,256]{1,0:T(8,128)(2,1)S(1)} collective-permute-done((bf16[736,256]{1,0:T(8,128)(2,1)}, bf16[736,256]{1,0:T(8,128)(2,1)S(1)}, u32[]{:S(2)}, u32[]{:S(2)}) %collective-permute-start.3) | collective-permute-done | bytes 376864 | tf_op jit(solution)/shard_map/ppermute | solution.py:72
  71.7 7.1 %all-to-all-done.1 = bf16[16,16,896]{2,1,0:T(8,128)(2,1)S(1)} async-done(((bf16[16,16,896]{2,1,0:T(8,128)(2,1)}), bf16[16,16,896]{2,1,0:T(8,128)(2,1)S(1)}, u32[]{:S(2)}, u32[]{:S(2)}) %all-to-all-start.1) | async-done | bytes 458784 | tf_op jit(solution)/shard_map/all_to_all | solution.py:326
  78.9 2.0 collective-permute-start.4
  80.9 7.4 %collective-permute-start.6 = (bf16[512,256]{1,0:T(8,128)(2,1)S(1)}, bf16[512,256]{1,0:T(8,128)(2,1)S(1)}, u32[]{:S(2)}, u32[]{:S(2)}) collective-permute-start(bf16[512,256]{1,0:T(8,128)(2,1)S(1)} %pad_maximum_fusion.5), channel_id=1, source_target_pairs={{0,0},{1,1},{2,2},{3,3},{4,4},{5,5},{6,6},{7,7},{8,8},{9,9},{10,10... | collective-permute-start | bytes 786440 | tf_op jit(solution)/shard_map/ppermute | solution.py:72
  88.3 7.0 %collective-permute-done.6 = bf16[512,256]{1,0:T(8,128)(2,1)S(1)} collective-permute-done((bf16[512,256]{1,0:T(8,128)(2,1)S(1)}, bf16[512,256]{1,0:T(8,128)(2,1)S(1)}, u32[]{:S(2)}, u32[]{:S(2)}) %collective-permute-start.6) | collective-permute-done | bytes 262176 | tf_op jit(solution)/shard_map/ppermute | solution.py:72
  95.4 3.2 %collective-permute-start.7 = (bf16[512,256]{1,0:T(8,128)(2,1)S(1)}, bf16[512,256]{1,0:T(8,128)(2,1)S(1)}, u32[]{:S(2)}, u32[]{:S(2)}) collective-permute-start(bf16[512,256]{1,0:T(8,128)(2,1)S(1)} %collective-permute-done.6), channel_id=1, source_target_pairs={{0,0},{1,1},{2,18},{3,19},{4,68},{5,69},{6,86},{7,87},{8,136},{9,1... | collective-permute-start | bytes 786440 | tf_op jit(solution)/shard_map/ppermute | solution.py:72
  98.5 1.9 copy-done.3
  100.5 5.7 %encode.2 = bf16[256,896]{1,0:T(8,128)(2,1)} custom-call(bf16[256,896]{1,0:T(8,128)(2,1)S(1)} %collective-permute-done.4.refs_0_, bf16[16,112,896]{2,1,0:T(8,128)(2,1)S(1)} %bitcast.25, bf16[16,112,896]{2,1,0:T(8,128)(2,1)S(1)} %bitcast.27), custom_call_target="tpu_custom_call" | custom-call | flops 1 | bytes 1 | tf_op jit(solution)/shard_map/encode/pallas_call | solution.py:182
  106.2 1.6 collective-permute-start.8
  109.9 5.0 %encode.3 = f32[256,896]{1,0:T(8,128)S(1)} custom-call(bf16[256,896]{1,0:T(8,128)(2,1)S(1)} %bitcast.32, bf16[16,112,896]{2,1,0:T(8,128)(2,1)S(1)} %bitcast.26, bf16[16,112,896]{2,1,0:T(8,128)(2,1)S(1)} %bitcast.28), custom_call_target="tpu_custom_call" | custom-call | flops 1 | bytes 1 | tf_op jit(solution)/shard_map/encode/pallas_call | solution.py:182
  116.9 5.8 %collective-permute-done.9 = bf16[64,4096]{1,0:T(8,128)(2,1)} collective-permute-done((bf16[64,4096]{1,0:T(8,128)(2,1)}, bf16[64,4096]{1,0:T(8,128)(2,1)}, u32[]{:S(2)}, u32[]{:S(2)}) %collective-permute-start.9) | collective-permute-done | bytes 524320 | tf_op jit(solution)/shard_map/ppermute | solution.py:72
  122.8 2.8 %all-gather.6.cloned.1.call-done = bf16[5888,256]{1,0:T(8,128)(2,1)} async-done(((bf16[736,256]{1,0:T(8,128)(2,1)}), bf16[5888,256]{1,0:T(8,128)(2,1)}) %all-gather.6.cloned.1.call-update) | async-done | bytes 3014672 | tf_op jit(solution)/shard_map/all_gather | solution.py:330
  125.6 1.9 pad_maximum_fusion
  127.5 1.8 collective-permute-start.12
  130.0 2.2 collective-permute-start.16
  132.2 1.3 collective-permute-start.11
  136.8 4.7 %collective-permute-done.18.refs_1_ = bf16[256,896]{1,0:T(8,128)(2,1)S(1)} collective-permute-done((bf16[256,896]{1,0:T(8,128)(2,1)S(1)}, bf16[256,896]{1,0:T(8,128)(2,1)S(1)}, u32[]{:S(2)}, u32[]{:S(2)}) %collective-permute-start.18) | collective-permute-done | bytes 458784 | tf_op jit(solution)/shard_map/ppermute | solution.py:72
  142.8 9.1 %collective-permute-start.19 = (bf16[256,896]{1,0:T(8,128)(2,1)S(1)}, bf16[256,896]{1,0:T(8,128)(2,1)S(1)}, u32[]{:S(2)}, u32[]{:S(2)}) collective-permute-start(bf16[256,896]{1,0:T(8,128)(2,1)S(1)} %collective-permute-done.18.refs_1_), channel_id=1, source_target_pairs={{0,16},{1,17},{2,18},{3,19},{4,20},{5,21},{6,22},{7,23},{8,24},{9,... | collective-permute-start | bytes 1376264 | tf_op jit(solution)/shard_map/ppermute | solution.py:72
  155.0 1.3 query.2.refs_0_
  156.2 1.7 attend.11.mixed_a
  157.9 1.7 attend.10.mixed_a
  159.6 1.6 attend.9.mixed_a
  161.2 1.6 attend.8.mixed_a
  162.9 1.3 query.3.refs_0_
  164.2 3.1 %collective-permute-done.20.refs_3_ = bf16[1792,256]{1,0:T(8,128)(2,1)S(1)} collective-permute-done((bf16[1792,256]{1,0:T(8,128)(2,1)S(1)}, bf16[1792,256]{1,0:T(8,128)(2,1)S(1)}, u32[]{:S(2)}, u32[]{:S(2)}) %collective-permute-start.20) | collective-permute-done | bytes 917536 | tf_op jit(solution)/shard_map/ppermute | solution.py:72
  167.3 1.6 attend.15.mixed_b
  168.9 1.7 attend.14.mixed_b
  170.6 1.7 attend.13.mixed_b
  172.2 1.7 attend.12.mixed_b
  173.9 5.5 %all-gather.8.cloned.1.call-done = bf16[8192,256]{1,0:T(8,128)(2,1)} async-done(((bf16[1024,256]{1,0:T(8,128)(2,1)}), bf16[8192,256]{1,0:T(8,128)(2,1)}) %all-gather.8.cloned.1.call-update) | async-done | bytes 4194320 | tf_op jit(solution)/shard_map/all_gather | solution.py:349
  179.4 2.2 copy-done.1
  181.5 1.3 project.4
  183.7 1.3 project.5
  185.1 1.3 project.6
  187.0 1.3 project.7
  188.6 3.0 %collective-permute-start.22 = (bf16[64,4096]{1,0:T(8,128)(2,1)S(1)}, bf16[64,4096]{1,0:T(8,128)(2,1)S(1)}, u32[]{:S(2)}, u32[]{:S(2)}) collective-permute-start(bf16[64,4096]{1,0:T(8,128)(2,1)S(1)} %add_convert_fusion.2), channel_id=1, source_target_pairs={{0,128},{1,129},{2,130},{3,131},{4,132},{5,133},{6,134},{7,135},{8... | collective-permute-start | bytes 1572872 | tf_op jit(solution)/shard_map/ppermute | solution.py:72
  193.4 10.0 %collective-permute-done.22 = bf16[64,4096]{1,0:T(8,128)(2,1)S(1)} collective-permute-done((bf16[64,4096]{1,0:T(8,128)(2,1)S(1)}, bf16[64,4096]{1,0:T(8,128)(2,1)S(1)}, u32[]{:S(2)}, u32[]{:S(2)}) %collective-permute-start.22) | collective-permute-done | bytes 524320 | tf_op jit(solution)/shard_map/ppermute | solution.py:72
  203.5 11.3 %collective-permute-done.24 = bf16[64,4096]{1,0:T(8,128)(2,1)S(1)} collective-permute-done((bf16[64,4096]{1,0:T(8,128)(2,1)S(1)}, bf16[64,4096]{1,0:T(8,128)(2,1)S(1)}, u32[]{:S(2)}, u32[]{:S(2)}) %collective-permute-start.24) | collective-permute-done | bytes 524320 | tf_op jit(solution)/shard_map/ppermute | solution.py:72
  (95 shorter events, 29.7 us)
Async XLA Ops:
  6.5 21.1 %copy-start = (bf16[4096,256]{1,0:T(8,128)(2,1)S(1)}, bf16[4096,256]{1,0:T(8,128)(2,1)}, u32[]{:S(2)}) copy-start(bf16[4096,256]{1,0:T(8,128)(2,1)} %param.10) | copy-start | bytes 6291460
  6.5 72.2 %all-gather.4.cloned.1.call-start = ((), (), s32[]{:S(2)}) async-start(), calls=%async_computation.2 | async-start | bytes 3612672 | tf_op jit(solution)/shard_map/all_gather | solution.py:301
  8.5 29.9 %copy-start.7 = (s32[512]{0:T(512)S(1)}, s32[512]{0:T(512)}, u32[]{:S(2)}) copy-start(s32[512]{0:T(512)} %param.17) | copy-start | bytes 6148
  11.8 43.6 %collective-permute-start.1 = (bf16[64,4096]{1,0:T(8,128)(2,1)}, bf16[64,4096]{1,0:T(8,128)(2,1)}, u32[]{:S(2)}, u32[]{:S(2)}) collective-permute-start(bf16[64,4096]{1,0:T(8,128)(2,1)} %fusion.2), channel_id=1, source_target_pairs={{0,64},{1,65},{2,66},{3,67},{4,68},{5,69},{6,70},{7,71},{8,72},{9,... | collective-permute-start | bytes 1572872 | tf_op jit(solution)/shard_map/ppermute | solution.py:72
  13.9 41.5 %collective-permute-start.2 = (bf16[64,4096]{1,0:T(8,128)(2,1)}, bf16[64,4096]{1,0:T(8,128)(2,1)}, u32[]{:S(2)}, u32[]{:S(2)}) collective-permute-start(bf16[64,4096]{1,0:T(8,128)(2,1)} %fusion.2), channel_id=1, source_target_pairs={{0,192},{1,193},{2,194},{3,195},{4,196},{5,197},{6,198},{7,199},{8... | collective-permute-start | bytes 1572872 | tf_op jit(solution)/shard_map/ppermute | solution.py:72
  20.7 20.0 %all-to-all-start = ((bf16[16,24,896]{2,1,0:T(8,128)(2,1)}), bf16[16,24,896]{2,1,0:T(8,128)(2,1)S(1)}, u32[]{:S(2)}, u32[]{:S(2)}) async-start(bf16[16,24,896]{2,1,0:T(8,128)(2,1)} %bitcast.2), calls=%async_computation | async-start | bytes 1376256 | tf_op jit(solution)/shard_map/all_to_all | solution.py:320
  29.6 25.9 %collective-permute-start = (bf16[736,256]{1,0:T(8,128)(2,1)}, bf16[736,256]{1,0:T(8,128)(2,1)}, u32[]{:S(2)}, u32[]{:S(2)}) collective-permute-start(bf16[736,256]{1,0:T(8,128)(2,1)} %pad_maximum_fusion.4), channel_id=1, source_target_pairs={{0,0},{1,1},{2,2},{3,3},{4,4},{5,5},{6,6},{7,7},{8,8},{9,9},{10,10... | collective-permute-start | bytes 1130504 | tf_op jit(solution)/shard_map/ppermute | solution.py:72
  55.5 23.3 %all-to-all-start.1 = ((bf16[16,16,896]{2,1,0:T(8,128)(2,1)}), bf16[16,16,896]{2,1,0:T(8,128)(2,1)S(1)}, u32[]{:S(2)}, u32[]{:S(2)}) async-start(bf16[16,16,896]{2,1,0:T(8,128)(2,1)} %bitcast.5), calls=%async_computation.1 | async-start | bytes 917504 | tf_op jit(solution)/shard_map/all_to_all | solution.py:326
  62.7 62.9 %all-gather.6.cloned.1.call-start = ((), (), s32[]{:S(2)}) async-start(), calls=%async_computation.3 | async-start | bytes 3391488 | tf_op jit(solution)/shard_map/all_gather | solution.py:330
  62.7 9.0 %collective-permute-start.3 = (bf16[736,256]{1,0:T(8,128)(2,1)}, bf16[736,256]{1,0:T(8,128)(2,1)S(1)}, u32[]{:S(2)}, u32[]{:S(2)}) collective-permute-start(bf16[736,256]{1,0:T(8,128)(2,1)} %collective-permute-done), channel_id=1, source_target_pairs={{0,0},{1,1},{2,18},{3,19},{4,68},{5,69},{6,86},{7,87},{8,136},{9,1... | collective-permute-start | bytes 1130504 | tf_op jit(solution)/shard_map/ppermute | solution.py:72
  71.7 7.1 %copy-start.6 = (bf16[736,256]{1,0:T(8,128)(2,1)}, bf16[736,256]{1,0:T(8,128)(2,1)S(1)}, u32[]{:S(2)}) copy-start(bf16[736,256]{1,0:T(8,128)(2,1)S(1)} %collective-permute-done.3) | copy-start | bytes 1130500
  78.8 100.6 %all-gather.8.cloned.1.call-start = ((), (), s32[]{:S(2)}) async-start(), calls=%async_computation.4 | async-start | bytes 4718592 | tf_op jit(solution)/shard_map/all_gather | solution.py:349
  78.8 16.5 %collective-permute-start.5 = (bf16[1792,896]{1,0:T(8,128)(2,1)}, bf16[1792,896]{1,0:T(8,128)(2,1)S(1)}, u32[]{:S(2)}, u32[]{:S(2)}) collective-permute-start(bf16[1792,896]{1,0:T(8,128)(2,1)} %all-gather.4.cloned.1.call-done), channel_id=1, source_target_pairs={{0,16},{1,17},{2,18},{3,19},{4,20},{5,21},{6,22},{7,23},{8,24},{9,... | collective-permute-start | bytes 9633800 | tf_op jit(solution)/shard_map/ppermute | solution.py:72
  78.9 16.4 %collective-permute-start.4 = (bf16[256,896]{1,0:T(8,128)(2,1)S(1)}, bf16[256,896]{1,0:T(8,128)(2,1)S(1)}, u32[]{:S(2)}, u32[]{:S(2)}) collective-permute-start(bf16[256,896]{1,0:T(8,128)(2,1)S(1)} %bitcast.31), channel_id=1, source_target_pairs={{0,1},{1,32},{2,3},{3,34},{4,5},{5,36},{6,7},{7,38},{8,9},{9,40},{... | collective-permute-start | bytes 1376264 | tf_op jit(solution)/shard_map/ppermute | solution.py:72
  80.9 14.4 %collective-permute-start.6 = (bf16[512,256]{1,0:T(8,128)(2,1)S(1)}, bf16[512,256]{1,0:T(8,128)(2,1)S(1)}, u32[]{:S(2)}, u32[]{:S(2)}) collective-permute-start(bf16[512,256]{1,0:T(8,128)(2,1)S(1)} %pad_maximum_fusion.5), channel_id=1, source_target_pairs={{0,0},{1,1},{2,2},{3,3},{4,4},{5,5},{6,6},{7,7},{8,8},{9,9},{10,10... | collective-permute-start | bytes 786440 | tf_op jit(solution)/shard_map/ppermute | solution.py:72
  95.4 10.8 %collective-permute-start.7 = (bf16[512,256]{1,0:T(8,128)(2,1)S(1)}, bf16[512,256]{1,0:T(8,128)(2,1)S(1)}, u32[]{:S(2)}, u32[]{:S(2)}) collective-permute-start(bf16[512,256]{1,0:T(8,128)(2,1)S(1)} %collective-permute-done.6), channel_id=1, source_target_pairs={{0,0},{1,1},{2,18},{3,19},{4,68},{5,69},{6,86},{7,87},{8,136},{9,1... | collective-permute-start | bytes 786440 | tf_op jit(solution)/shard_map/ppermute | solution.py:72
  98.5 1.9 copy-start.3
  106.2 9.6 %collective-permute-start.8 = (bf16[256,896]{1,0:T(8,128)(2,1)}, bf16[256,896]{1,0:T(8,128)(2,1)}, u32[]{:S(2)}, u32[]{:S(2)}) collective-permute-start(bf16[256,896]{1,0:T(8,128)(2,1)} %encode.2), channel_id=1, source_target_pairs={{0,33},{1,0},{2,35},{3,2},{4,37},{5,4},{6,39},{7,6},{8,41},{9,8},{... | collective-permute-start | bytes 1376264 | tf_op jit(solution)/shard_map/ppermute | solution.py:72
  107.8 7.1 %collective-permute-start.10 = (bf16[512,256]{1,0:T(8,128)(2,1)S(1)}, bf16[512,256]{1,0:T(8,128)(2,1)S(1)}, u32[]{:S(2)}, u32[]{:S(2)}) collective-permute-start(bf16[512,256]{1,0:T(8,128)(2,1)S(1)} %collective-permute-done.7), channel_id=1, source_target_pairs={{0,1},{1,32},{2,3},{3,34},{4,5},{5,36},{6,7},{7,38},{8,9},{9,40},{... | collective-permute-start | bytes 786440 | tf_op jit(solution)/shard_map/ppermute | solution.py:72
  108.9 13.9 %collective-permute-start.9 = (bf16[64,4096]{1,0:T(8,128)(2,1)}, bf16[64,4096]{1,0:T(8,128)(2,1)}, u32[]{:S(2)}, u32[]{:S(2)}) collective-permute-start(bf16[64,4096]{1,0:T(8,128)(2,1)} %fusion.2), channel_id=1, source_target_pairs={{0,128},{1,129},{2,130},{3,131},{4,132},{5,133},{6,134},{7,135},{8... | collective-permute-start | bytes 1572872 | tf_op jit(solution)/shard_map/ppermute | solution.py:72
  125.6 3.7 %copy-start.5 = (bf16[5888,256]{1,0:T(8,128)(2,1)S(1)}, bf16[5888,256]{1,0:T(8,128)(2,1)}, u32[]{:S(2)}) copy-start(bf16[5888,256]{1,0:T(8,128)(2,1)} %all-gather.6.cloned.1.call-done) | copy-start | bytes 9043972
  127.5 26.9 %collective-permute-start.12 = (bf16[256,4096]{1,0:T(8,128)(2,1)S(1)}, bf16[256,4096]{1,0:T(8,128)(2,1)S(1)}, u32[]{:S(2)}, u32[]{:S(2)}) collective-permute-start(bf16[256,4096]{1,0:T(8,128)(2,1)S(1)} %pad_maximum_fusion), channel_id=1, source_target_pairs={{0,16},{1,17},{2,18},{3,19},{4,20},{5,21},{6,22},{7,23},{8,24},{9,... | collective-permute-start | bytes 6291464 | tf_op jit(solution)/shard_map/ppermute | solution.py:72
  129.5 11.9 %collective-permute-start.18 = (bf16[256,896]{1,0:T(8,128)(2,1)S(1)}, bf16[256,896]{1,0:T(8,128)(2,1)S(1)}, u32[]{:S(2)}, u32[]{:S(2)}) collective-permute-start(bf16[256,896]{1,0:T(8,128)(2,1)S(1)} %add_convert_fusion.3.refs_1_), channel_id=1, source_target_pairs={{0,192},{1,193},{2,194},{3,195},{4,196},{5,197},{6,198},{7,199},{8... | collective-permute-start | bytes 1376264 | tf_op jit(solution)/shard_map/ppermute | solution.py:72
  130.0 12.8 %collective-permute-start.16 = (bf16[256,896]{1,0:T(8,128)(2,1)S(1)}, bf16[256,896]{1,0:T(8,128)(2,1)S(1)}, u32[]{:S(2)}, u32[]{:S(2)}) collective-permute-start(bf16[256,896]{1,0:T(8,128)(2,1)S(1)} %add_convert_fusion.3.refs_1_), channel_id=1, source_target_pairs={{0,128},{1,129},{2,130},{3,131},{4,132},{5,133},{6,134},{7,135},{8... | collective-permute-start | bytes 1376264 | tf_op jit(solution)/shard_map/ppermute | solution.py:72
  132.2 21.7 %collective-permute-start.14 = (bf16[256,896]{1,0:T(8,128)(2,1)S(1)}, bf16[256,896]{1,0:T(8,128)(2,1)S(1)}, u32[]{:S(2)}, u32[]{:S(2)}) collective-permute-start(bf16[256,896]{1,0:T(8,128)(2,1)S(1)} %add_convert_fusion.3.refs_1_), channel_id=1, source_target_pairs={{0,64},{1,65},{2,66},{3,67},{4,68},{5,69},{6,70},{7,71},{8,72},{9,... | collective-permute-start | bytes 1376264 | tf_op jit(solution)/shard_map/ppermute | solution.py:72
  132.2 30.7 %collective-permute-start.11 = (bf16[4096,256]{1,0:T(8,128)(2,1)S(1)}, bf16[4096,256]{1,0:T(8,128)(2,1)S(1)}, u32[]{:S(2)}, u32[]{:S(2)}) collective-permute-start(bf16[4096,256]{1,0:T(8,128)(2,1)S(1)} %bitcast.29), channel_id=1, source_target_pairs={{0,1},{1,32},{2,3},{3,34},{4,5},{5,36},{6,7},{7,38},{8,9},{9,40},{... | collective-permute-start | bytes 6291464 | tf_op jit(solution)/shard_map/ppermute | solution.py:72
  141.5 25.8 %collective-permute-start.20 = (bf16[1792,256]{1,0:T(8,128)(2,1)S(1)}, bf16[1792,256]{1,0:T(8,128)(2,1)S(1)}, u32[]{:S(2)}, u32[]{:S(2)}) collective-permute-start(bf16[1792,256]{1,0:T(8,128)(2,1)S(1)} %pad_maximum_fusion.1.refs_3_), channel_id=1, source_target_pairs={{0,1},{1,32},{2,3},{3,34},{4,5},{5,36},{6,7},{7,38},{8,9},{9,40},{... | collective-permute-start | bytes 2752520 | tf_op jit(solution)/shard_map/ppermute | solution.py:72
  142.8 11.5 %collective-permute-start.19 = (bf16[256,896]{1,0:T(8,128)(2,1)S(1)}, bf16[256,896]{1,0:T(8,128)(2,1)S(1)}, u32[]{:S(2)}, u32[]{:S(2)}) collective-permute-start(bf16[256,896]{1,0:T(8,128)(2,1)S(1)} %collective-permute-done.18.refs_1_), channel_id=1, source_target_pairs={{0,16},{1,17},{2,18},{3,19},{4,20},{5,21},{6,22},{7,23},{8,24},{9,... | collective-permute-start | bytes 1376264 | tf_op jit(solution)/shard_map/ppermute | solution.py:72
  153.9 7.4 %collective-permute-start.13 = (bf16[256,896]{1,0:T(8,128)(2,1)S(1)}, bf16[256,896]{1,0:T(8,128)(2,1)S(1)}, u32[]{:S(2)}, u32[]{:S(2)}) collective-permute-start(bf16[256,896]{1,0:T(8,128)(2,1)S(1)} %add_convert_fusion.3.refs_1_), channel_id=1, source_target_pairs={{0,16},{1,17},{2,18},{3,19},{4,20},{5,21},{6,22},{7,23},{8,24},{9,... | collective-permute-start | bytes 1376264 | tf_op jit(solution)/shard_map/ppermute | solution.py:72
  154.2 3.7 %collective-permute-start.17 = (bf16[256,896]{1,0:T(8,128)(2,1)S(1)}, bf16[256,896]{1,0:T(8,128)(2,1)S(1)}, u32[]{:S(2)}, u32[]{:S(2)}) collective-permute-start(bf16[256,896]{1,0:T(8,128)(2,1)S(1)} %collective-permute-done.16.refs_1_), channel_id=1, source_target_pairs={{0,16},{1,17},{2,18},{3,19},{4,20},{5,21},{6,22},{7,23},{8,24},{9,... | collective-permute-start | bytes 1376264 | tf_op jit(solution)/shard_map/ppermute | solution.py:72
  154.4 5.2 %collective-permute-start.15 = (bf16[256,896]{1,0:T(8,128)(2,1)S(1)}, bf16[256,896]{1,0:T(8,128)(2,1)S(1)}, u32[]{:S(2)}, u32[]{:S(2)}) collective-permute-start(bf16[256,896]{1,0:T(8,128)(2,1)S(1)} %collective-permute-done.14.refs_1_), channel_id=1, source_target_pairs={{0,16},{1,17},{2,18},{3,19},{4,20},{5,21},{6,22},{7,23},{8,24},{9,... | collective-permute-start | bytes 1376264 | tf_op jit(solution)/shard_map/ppermute | solution.py:72
  179.4 2.2 copy-start.1
  182.9 4.1 %copy-start.2 = (bf16[8192,256]{1,0:T(8,128)(2,1)S(1)}, bf16[8192,256]{1,0:T(8,128)(2,1)}, u32[]{:S(2)}) copy-start(bf16[8192,256]{1,0:T(8,128)(2,1)} %all-gather.8.cloned.1.call-done) | copy-start | bytes 12582916
  182.9 5.6 %collective-permute-start.21 = (bf16[64,4096]{1,0:T(8,128)(2,1)S(1)}, bf16[64,4096]{1,0:T(8,128)(2,1)S(1)}, u32[]{:S(2)}, u32[]{:S(2)}) collective-permute-start(bf16[64,4096]{1,0:T(8,128)(2,1)S(1)} %get-tuple-element.80), channel_id=1, source_target_pairs={{0,16},{1,17},{2,18},{3,19},{4,20},{5,21},{6,22},{7,23},{8,24},{9,... | collective-permute-start | bytes 1572872 | tf_op jit(solution)/shard_map/ppermute | solution.py:72
  185.0 6.6 %collective-permute-start.23 = (bf16[64,4096]{1,0:T(8,128)(2,1)S(1)}, bf16[64,4096]{1,0:T(8,128)(2,1)S(1)}, u32[]{:S(2)}, u32[]{:S(2)}) collective-permute-start(bf16[64,4096]{1,0:T(8,128)(2,1)S(1)} %get-tuple-element.84), channel_id=1, source_target_pairs={{0,16},{1,17},{2,18},{3,19},{4,20},{5,21},{6,22},{7,23},{8,24},{9,... | collective-permute-start | bytes 1572872 | tf_op jit(solution)/shard_map/ppermute | solution.py:72
  186.4 6.2 %collective-permute-start.25 = (bf16[64,4096]{1,0:T(8,128)(2,1)S(1)}, bf16[64,4096]{1,0:T(8,128)(2,1)S(1)}, u32[]{:S(2)}, u32[]{:S(2)}) collective-permute-start(bf16[64,4096]{1,0:T(8,128)(2,1)S(1)} %get-tuple-element.88), channel_id=1, source_target_pairs={{0,16},{1,17},{2,18},{3,19},{4,20},{5,21},{6,22},{7,23},{8,24},{9,... | collective-permute-start | bytes 1572872 | tf_op jit(solution)/shard_map/ppermute | solution.py:72
  188.3 27.1 %copy-start.4 = (bf16[64,4096]{1,0:T(8,128)(2,1)S(1)}, bf16[64,4096]{1,0:T(8,128)(2,1)}, u32[]{:S(2)}) copy-start(bf16[64,4096]{1,0:T(8,128)(2,1)} %param.9) | copy-start | bytes 1572868
  188.3 5.1 %collective-permute-start.27 = (bf16[64,4096]{1,0:T(8,128)(2,1)S(1)}, bf16[64,4096]{1,0:T(8,128)(2,1)S(1)}, u32[]{:S(2)}, u32[]{:S(2)}) collective-permute-start(bf16[64,4096]{1,0:T(8,128)(2,1)S(1)} %get-tuple-element.92), channel_id=1, source_target_pairs={{0,16},{1,17},{2,18},{3,19},{4,20},{5,21},{6,22},{7,23},{8,24},{9,... | collective-permute-start | bytes 1572872 | tf_op jit(solution)/shard_map/ppermute | solution.py:72
  188.6 14.9 %collective-permute-start.22 = (bf16[64,4096]{1,0:T(8,128)(2,1)S(1)}, bf16[64,4096]{1,0:T(8,128)(2,1)S(1)}, u32[]{:S(2)}, u32[]{:S(2)}) collective-permute-start(bf16[64,4096]{1,0:T(8,128)(2,1)S(1)} %add_convert_fusion.2), channel_id=1, source_target_pairs={{0,128},{1,129},{2,130},{3,131},{4,132},{5,133},{6,134},{7,135},{8... | collective-permute-start | bytes 1572872 | tf_op jit(solution)/shard_map/ppermute | solution.py:72
  191.7 23.0 %collective-permute-start.24 = (bf16[64,4096]{1,0:T(8,128)(2,1)S(1)}, bf16[64,4096]{1,0:T(8,128)(2,1)S(1)}, u32[]{:S(2)}, u32[]{:S(2)}) collective-permute-start(bf16[64,4096]{1,0:T(8,128)(2,1)S(1)} %add_convert_fusion.1), channel_id=1, source_target_pairs={{0,192},{1,193},{2,194},{3,195},{4,196},{5,197},{6,198},{7,199},{8... | collective-permute-start | bytes 1572872 | tf_op jit(solution)/shard_map/ppermute | solution.py:72
  192.8 22.7 %collective-permute-start.26 = (bf16[64,4096]{1,0:T(8,128)(2,1)S(1)}, bf16[64,4096]{1,0:T(8,128)(2,1)S(1)}, u32[]{:S(2)}, u32[]{:S(2)}) collective-permute-start(bf16[64,4096]{1,0:T(8,128)(2,1)S(1)} %add_convert_fusion), channel_id=1, source_target_pairs={{0,64},{1,65},{2,66},{3,67},{4,68},{5,69},{6,70},{7,71},{8,72},{9,... | collective-permute-start | bytes 1572872 | tf_op jit(solution)/shard_map/ppermute | solution.py:72
Sparse Core Ops, SparseCore 0:
  9.1 66.7 all-gather.3
  78.9 46.6 all-gather.5
  127.4 51.9 all-gather.7

commit v2 on v1

--- a/solution.py
+++ b/solution.py
@@ -316,37 +316,39 @@
     )
     normed = rms_normed(hidden_states)
 
+    in_piece = send(in_piece, along_z(steps_a))
     packed, placing = pack(neighbours, counts, slot_of)
+
+    packed, in_piece, out_piece = together(packed, in_piece, out_piece)
     arrived = lax.all_to_all(packed, ("y", "xh", "core"), split_axis=0, concat_axis=0, tiled=True)
-    in_piece = send(in_piece, along_z(steps_a))
+    in_piece = send(in_piece, to_member(steps_a))
+    out_piece = send(out_piece, along_z(steps_b))
+    placed = place(arrived, placing)
+
+    placed, in_piece, out_piece, normed = together(placed, in_piece, out_piece, normed)
+    rows = lax.all_to_all(placed, ("z", "xl"), split_axis=0, concat_axis=0, tiled=True)
+    gathered = lax.all_gather(in_piece, "z", axis=0, tiled=True)
+    out_piece = send(out_piece, to_member(steps_b))
     token_1, token_3 = send(normed, Y_UP[1]), send(normed, Y_UP[3])
-    placed = place(arrived, placing)
-
-    placed, in_piece, token_1, token_3 = together(placed, in_piece, token_1, token_3)
-    rows = lax.all_to_all(placed, ("z", "xl"), split_axis=0, concat_axis=0, tiled=True)
-    in_piece = send(in_piece, to_member(steps_a))
-
-    rows, in_piece, out_piece, enc_a, normed = together(rows, in_piece, out_piece, enc_a, normed)
-    gathered = lax.all_gather(in_piece, "z", axis=0, tiled=True)
+
+    rows, out_piece, enc_a, normed = together(rows, out_piece, enc_a, normed)
     visitors = send(rows, X_OUT)
     enc_b = send(enc_a, CORE)
-    out_piece = send(out_piece, along_z(steps_b))
     token_2 = send(normed, Y_UP[2])
-
-    visitors, enc_b, out_piece = together(visitors, enc_b, out_piece)
-    out_piece = send(out_piece, to_member(steps_b))
+    out_other = send(out_piece, X_OUT)
+    visitors, enc_b, out_piece, out_other = together(visitors, enc_b, out_piece, out_other)
+    out_pieces = jnp.concatenate([out_piece, out_other], axis=0)
+    out_weight = lax.all_gather(out_pieces, "z", axis=0, tiled=True)
     visited = encode(visitors, enc_a, enc_b, keep_raw=False)
 
-    visited, rows, out_piece = together(visited, rows, out_piece)
+    visited, rows = together(visited, rows)
     returned = send(visited, X_BACK)
-    out_pieces = jnp.concatenate([out_piece, send(out_piece, X_OUT)], axis=0)
     encoded = encode(rows, enc_a, enc_b, keep_raw=True)
     encoded = (encoded + returned.astype(jnp.float32)).astype(jnp.bfloat16)
 
-    encoded, normed, token_1, token_2, token_3, out_pieces, gathered = together(
-        encoded, normed, token_1, token_2, token_3, out_pieces, gathered
-    )
-    out_weight = lax.all_gather(out_pieces, "z", axis=0, tiled=True)
+    encoded, normed, token_1, token_2, token_3, gathered = together(
+        encoded, normed, token_1, token_2, token_3, gathered
+    )
     blocks = [encoded] + [send(encoded, Y_UP[d]) for d in (1, 2, 3)]
     parts = gathered.reshape(8, -1, width)
     q_rows, k_rows = query_weight.shape[0] // 8, feat // 8

time: 224 us -> 238 us (1.062)
  starting transfers between devices: 69.5 us -> 79.4 us
  local copies, waits for them, and re-layouts: 15.3 us -> 20.2 us
  other arithmetic: 12.2 us -> 9.35 us
    ppermute x28, waiting for transfers between devices: 61.2 us -> 74.9 us  [send(): return lax.ppermute(x, AXES, perm)]
    all_to_all x1, starting transfers between devices: 6.91 us -> 13.9 us  [body(): lax.all_to_all(packed, ('y', 'xh', 'core'), split_axis=0, concat_axis=0,...]
    ppermute x28, starting transfers between devices: 55.3 us -> 61.3 us  [send(): return lax.ppermute(x, AXES, perm)]
    all_gather x1, waiting for transfers between devices: 5.46 us -> 0.02 us  [body(): out_weight = lax.all_gather(out_pieces, 'z', axis=0, tiled=True)]
    all_to_all x1, starting transfers between devices: 7.2 us -> 4.07 us  [body(): lax.all_to_all(placed, ('z', 'xl'), split_axis=0, concat_axis=0, tiled=True)]
    all_gather x1, waiting for transfers between devices: 2.81 us -> 0.01 us  [body(): gathered = lax.all_gather(in_piece, 'z', axis=0, tiled=True)]
    unnamed x20 -> x28, local copies, waits for them, and re-layouts: 8.5 us -> 11.1 us
  transfers between devices with their start and end apart: 33 -> 33, of which waited for: 15 -> 14; matrix products, arithmetic and copies ran while one was open for 10% -> 9% of each run, Pallas kernels for 14% -> 13%
where the time goes in v2:
time: 238 us; the launch traced here: 237 us
  waiting for transfers between devices  80.5 us (34%)
  starting transfers between devices  79.4 us (33%)
  Pallas kernels  31 us (13%)
  local copies, waits for them, and re-layouts  20.2 us (8%)
  between operations  13.7 us (6%)
  other arithmetic  9.35 us (4%)
  matrix products  2.76 us (1%)
    ppermute x28, waiting for transfers between devices, send(): return lax.ppermute(x, AXES, perm)  74.9 us
    ppermute x28, starting transfers between devices, send(): return lax.ppermute(x, AXES, perm)  61.3 us
    all_to_all x1, starting transfers between devices, body(): lax.all_to_all(packed, ('y', 'xh', 'core'), split_axis=0, concat_axis=0,...  13.9 us
    pallas_call x8, Pallas kernels, attend(): pl.pallas_call(lambda *refs: attend_kernel(first, *refs), out_shape=jax.S...  13.2 us
    unnamed x28, local copies, waits for them, and re-layouts  11.1 us
    pallas_call x2, Pallas kernels, encode(): pl.pallas_call(lambda *refs: encode_kernel(steps, keep_raw, *refs), grid=...  10 us
    all_to_all x1, waiting for transfers between devices, body(): lax.all_to_all(placed, ('z', 'xl'), split_axis=0, concat_axis=0, tiled=True)  5.52 us
    pallas_call x4, Pallas kernels, project(): pl.pallas_call(project_kernel, grid=(steps,), in_specs=[rows, rows, pl.Bl...  5.31 us
  transfers between devices with their start and end apart: 33, of which 14 were waited for; matrix products, arithmetic and copies ran while one was open for 9% of the time, Pallas kernels for 13%

profile of v2, /device:TPU:1, one launch (start us, length us, event | category | flops | bytes accessed | tf_op | source)
XLA Modules:
  0.0 236.9 jit_solution(2115079878528984127)
XLA Ops:
  10.7 9.6 %collective-permute-start = (bf16[736,256]{1,0:T(8,128)(2,1)}, bf16[736,256]{1,0:T(8,128)(2,1)}, u32[]{:S(2)}, u32[]{:S(2)}) collective-permute-start(bf16[736,256]{1,0:T(8,128)(2,1)} %pad_maximum_fusion.4), channel_id=1, source_target_pairs={{0,0},{1,1},{2,2},{3,3},{4,4},{5,5},{6,6},{7,7},{8,8},{9,9},{10,10... | collective-permute-start | bytes 1130504 | tf_op jit(solution)/shard_map/ppermute | solution.py:72
  20.9 1.6 constant_dynamic-slice_fusion.6
  24.4 1.6 pad_maximum_fusion.5
  27.3 2.7 %collective-permute-done = bf16[736,256]{1,0:T(8,128)(2,1)} collective-permute-done((bf16[736,256]{1,0:T(8,128)(2,1)}, bf16[736,256]{1,0:T(8,128)(2,1)}, u32[]{:S(2)}, u32[]{:S(2)}) %collective-permute-start) | collective-permute-done | bytes 376864 | tf_op jit(solution)/shard_map/ppermute | solution.py:72
  30.0 13.9 %all-to-all-start = ((bf16[16,24,896]{2,1,0:T(8,128)(2,1)}), bf16[16,24,896]{2,1,0:T(8,128)(2,1)}, u32[]{:S(2)}, u32[]{:S(2)}) async-start(bf16[16,24,896]{2,1,0:T(8,128)(2,1)} %bitcast.5), calls=%async_computation | async-start | bytes 1376256 | tf_op jit(solution)/shard_map/all_to_all | solution.py:323
  44.1 5.0 %collective-permute-start.1 = (bf16[736,256]{1,0:T(8,128)(2,1)}, bf16[736,256]{1,0:T(8,128)(2,1)}, u32[]{:S(2)}, u32[]{:S(2)}) collective-permute-start(bf16[736,256]{1,0:T(8,128)(2,1)} %collective-permute-done), channel_id=1, source_target_pairs={{0,0},{1,1},{2,18},{3,19},{4,68},{5,69},{6,86},{7,87},{8,136},{9,1... | collective-permute-start | bytes 1130504 | tf_op jit(solution)/shard_map/ppermute | solution.py:72
  49.2 8.0 %collective-permute-start.2 = (bf16[512,256]{1,0:T(8,128)(2,1)}, bf16[512,256]{1,0:T(8,128)(2,1)}, u32[]{:S(2)}, u32[]{:S(2)}) collective-permute-start(bf16[512,256]{1,0:T(8,128)(2,1)} %pad_maximum_fusion.5), channel_id=1, source_target_pairs={{0,0},{1,1},{2,2},{3,3},{4,4},{5,5},{6,6},{7,7},{8,8},{9,9},{10,10... | collective-permute-start | bytes 786440 | tf_op jit(solution)/shard_map/ppermute | solution.py:72
  59.8 2.0 reshape.98
  61.8 6.8 %collective-permute-done.2 = bf16[512,256]{1,0:T(8,128)(2,1)} collective-permute-done((bf16[512,256]{1,0:T(8,128)(2,1)}, bf16[512,256]{1,0:T(8,128)(2,1)}, u32[]{:S(2)}, u32[]{:S(2)}) %collective-permute-start.2) | collective-permute-done | bytes 262176 | tf_op jit(solution)/shard_map/ppermute | solution.py:72
  68.6 4.1 %all-to-all-start.1 = ((bf16[16,16,896]{2,1,0:T(8,128)(2,1)}), bf16[16,16,896]{2,1,0:T(8,128)(2,1)S(1)}, u32[]{:S(2)}, u32[]{:S(2)}) async-start(bf16[16,16,896]{2,1,0:T(8,128)(2,1)} %bitcast.6), calls=%async_computation.1 | async-start | bytes 917504 | tf_op jit(solution)/shard_map/all_to_all | solution.py:329
  72.8 5.3 %collective-permute-start.3 = (bf16[512,256]{1,0:T(8,128)(2,1)}, bf16[512,256]{1,0:T(8,128)(2,1)S(1)}, u32[]{:S(2)}, u32[]{:S(2)}) collective-permute-start(bf16[512,256]{1,0:T(8,128)(2,1)} %collective-permute-done.2), channel_id=1, source_target_pairs={{0,0},{1,1},{2,18},{3,19},{4,68},{5,69},{6,86},{7,87},{8,136},{9,1... | collective-permute-start | bytes 786440 | tf_op jit(solution)/shard_map/ppermute | solution.py:72
  78.1 3.7 %collective-permute-done.3 = bf16[512,256]{1,0:T(8,128)(2,1)S(1)} collective-permute-done((bf16[512,256]{1,0:T(8,128)(2,1)}, bf16[512,256]{1,0:T(8,128)(2,1)S(1)}, u32[]{:S(2)}, u32[]{:S(2)}) %collective-permute-start.3) | collective-permute-done | bytes 262176 | tf_op jit(solution)/shard_map/ppermute | solution.py:72
  81.8 5.5 %all-to-all-done.1 = bf16[16,16,896]{2,1,0:T(8,128)(2,1)S(1)} async-done(((bf16[16,16,896]{2,1,0:T(8,128)(2,1)}), bf16[16,16,896]{2,1,0:T(8,128)(2,1)S(1)}, u32[]{:S(2)}, u32[]{:S(2)}) %all-to-all-start.1) | async-done | bytes 458784 | tf_op jit(solution)/shard_map/all_to_all | solution.py:329
  87.3 3.5 %collective-permute-start.5 = (bf16[1792,896]{1,0:T(8,128)(2,1)}, bf16[1792,896]{1,0:T(8,128)(2,1)S(1)}, u32[]{:S(2)}, u32[]{:S(2)}) collective-permute-start(bf16[1792,896]{1,0:T(8,128)(2,1)} %all-gather.4.cloned.1.call-done), channel_id=1, source_target_pairs={{0,16},{1,17},{2,18},{3,19},{4,20},{5,21},{6,22},{7,23},{8,24},{9,... | collective-permute-start | bytes 9633800 | tf_op jit(solution)/shard_map/ppermute | solution.py:72
  90.7 2.5 %collective-permute-start.6 = (bf16[512,256]{1,0:T(8,128)(2,1)}, bf16[512,256]{1,0:T(8,128)(2,1)S(1)}, u32[]{:S(2)}, u32[]{:S(2)}) collective-permute-start(bf16[512,256]{1,0:T(8,128)(2,1)} %copy-done.9), channel_id=1, source_target_pairs={{0,1},{1,32},{2,3},{3,34},{4,5},{5,36},{6,7},{7,38},{8,9},{9,40},{... | collective-permute-start | bytes 786440 | tf_op jit(solution)/shard_map/ppermute | solution.py:72
  93.2 8.1 %collective-permute-done.6 = bf16[512,256]{1,0:T(8,128)(2,1)S(1)} collective-permute-done((bf16[512,256]{1,0:T(8,128)(2,1)}, bf16[512,256]{1,0:T(8,128)(2,1)S(1)}, u32[]{:S(2)}, u32[]{:S(2)}) %collective-permute-start.6) | collective-permute-done | bytes 262176 | tf_op jit(solution)/shard_map/ppermute | solution.py:72
  101.3 1.8 copy-done.4
  103.1 1.8 pad_maximum_fusion.2
  104.9 1.9 copy-done.3
  106.8 1.9 copy-done.5
  108.8 5.0 %encode.2 = bf16[256,896]{1,0:T(8,128)(2,1)S(1)} custom-call(bf16[256,896]{1,0:T(8,128)(2,1)S(1)} %collective-permute-done.4.refs_0_, bf16[16,112,896]{2,1,0:T(8,128)(2,1)S(1)} %bitcast.28, bf16[16,112,896]{2,1,0:T(8,128)(2,1)S(1)} %bitcast.30), custom_call_target="tpu_custom_call" | custom-call | flops 1 | bytes 1 | tf_op jit(solution)/shard_map/encode/pallas_call | solution.py:182
  114.2 2.7 %collective-permute-start.10 = (bf16[64,4096]{1,0:T(8,128)(2,1)S(1)}, bf16[64,4096]{1,0:T(8,128)(2,1)}, u32[]{:S(2)}, u32[]{:S(2)}) collective-permute-start(bf16[64,4096]{1,0:T(8,128)(2,1)S(1)} %fusion.2), channel_id=1, source_target_pairs={{0,192},{1,193},{2,194},{3,195},{4,196},{5,197},{6,198},{7,199},{8... | collective-permute-start | bytes 1572872 | tf_op jit(solution)/shard_map/ppermute | solution.py:72
  117.0 3.1 %collective-permute-start.9 = (bf16[64,4096]{1,0:T(8,128)(2,1)S(1)}, bf16[64,4096]{1,0:T(8,128)(2,1)}, u32[]{:S(2)}, u32[]{:S(2)}) collective-permute-start(bf16[64,4096]{1,0:T(8,128)(2,1)S(1)} %fusion.2), channel_id=1, source_target_pairs={{0,128},{1,129},{2,130},{3,131},{4,132},{5,133},{6,134},{7,135},{8... | collective-permute-start | bytes 1572872 | tf_op jit(solution)/shard_map/ppermute | solution.py:72
  120.0 5.0 %encode.3 = f32[256,896]{1,0:T(8,128)S(1)} custom-call(bf16[256,896]{1,0:T(8,128)(2,1)S(1)} %bitcast.35, bf16[16,112,896]{2,1,0:T(8,128)(2,1)S(1)} %bitcast.29, bf16[16,112,896]{2,1,0:T(8,128)(2,1)S(1)} %bitcast.31), custom_call_target="tpu_custom_call" | custom-call | flops 1 | bytes 1 | tf_op jit(solution)/shard_map/encode/pallas_call | solution.py:182
  125.2 2.0 collective-permute-done.10
  127.2 2.8 %collective-permute-done.8 = bf16[64,4096]{1,0:T(8,128)(2,1)} collective-permute-done((bf16[64,4096]{1,0:T(8,128)(2,1)S(1)}, bf16[64,4096]{1,0:T(8,128)(2,1)}, u32[]{:S(2)}, u32[]{:S(2)}) %collective-permute-start.8) | collective-permute-done | bytes 524320 | tf_op jit(solution)/shard_map/ppermute | solution.py:72
  130.0 11.5 %collective-permute-done.9 = bf16[64,4096]{1,0:T(8,128)(2,1)} collective-permute-done((bf16[64,4096]{1,0:T(8,128)(2,1)S(1)}, bf16[64,4096]{1,0:T(8,128)(2,1)}, u32[]{:S(2)}, u32[]{:S(2)}) %collective-permute-start.9) | collective-permute-done | bytes 524320 | tf_op jit(solution)/shard_map/ppermute | solution.py:72
  141.5 1.7 pad_maximum_fusion
  143.3 2.8 %collective-permute-start.12 = (bf16[256,4096]{1,0:T(8,128)(2,1)S(1)}, bf16[256,4096]{1,0:T(8,128)(2,1)S(1)}, u32[]{:S(2)}, u32[]{:S(2)}) collective-permute-start(bf16[256,4096]{1,0:T(8,128)(2,1)S(1)} %pad_maximum_fusion), channel_id=1, source_target_pairs={{0,16},{1,17},{2,18},{3,19},{4,20},{5,21},{6,22},{7,23},{8,24},{9,... | collective-permute-start | bytes 6291464 | tf_op jit(solution)/shard_map/ppermute | solution.py:72
  148.0 1.8 collective-permute-start.11
  152.0 6.1 %collective-permute-done.18.refs_1_ = bf16[256,896]{1,0:T(8,128)(2,1)S(1)} collective-permute-done((bf16[256,896]{1,0:T(8,128)(2,1)S(1)}, bf16[256,896]{1,0:T(8,128)(2,1)S(1)}, u32[]{:S(2)}, u32[]{:S(2)}) %collective-permute-start.18) | collective-permute-done | bytes 458784 | tf_op jit(solution)/shard_map/ppermute | solution.py:72
  158.2 1.8 collective-permute-start.20
  160.0 2.2 collective-permute-start.19
  163.3 7.2 %collective-permute-done.14.refs_1_ = bf16[256,896]{1,0:T(8,128)(2,1)S(1)} collective-permute-done((bf16[256,896]{1,0:T(8,128)(2,1)S(1)}, bf16[256,896]{1,0:T(8,128)(2,1)S(1)}, u32[]{:S(2)}, u32[]{:S(2)}) %collective-permute-start.14) | collective-permute-done | bytes 458784 | tf_op jit(solution)/shard_map/ppermute | solution.py:72
  172.9 1.7 attend.11.mixed_a
  174.6 1.7 attend.10.mixed_a
  176.2 1.6 attend.9.mixed_a
  177.9 1.7 attend.8.mixed_a
  180.8 2.2 collective-permute-done.20.refs_3_
  183.0 1.6 attend.15.mixed_b
  184.7 1.6 attend.14.mixed_b
  186.3 1.7 attend.13.mixed_b
  188.0 1.7 attend.12.mixed_b
  189.7 2.2 copy-done.1
  193.2 3.3 %collective-permute-start.21 = (bf16[64,4096]{1,0:T(8,128)(2,1)S(1)}, bf16[64,4096]{1,0:T(8,128)(2,1)S(1)}, u32[]{:S(2)}, u32[]{:S(2)}) collective-permute-start(bf16[64,4096]{1,0:T(8,128)(2,1)S(1)} %get-tuple-element.82), channel_id=1, source_target_pairs={{0,16},{1,17},{2,18},{3,19},{4,20},{5,21},{6,22},{7,23},{8,24},{9,... | collective-permute-start | bytes 1572872 | tf_op jit(solution)/shard_map/ppermute | solution.py:72
  201.4 4.2 %collective-permute-start.22 = (bf16[64,4096]{1,0:T(8,128)(2,1)S(1)}, bf16[64,4096]{1,0:T(8,128)(2,1)S(1)}, u32[]{:S(2)}, u32[]{:S(2)}) collective-permute-start(bf16[64,4096]{1,0:T(8,128)(2,1)S(1)} %add_convert_fusion.2), channel_id=1, source_target_pairs={{0,128},{1,129},{2,130},{3,131},{4,132},{5,133},{6,134},{7,135},{8... | collective-permute-start | bytes 1572872 | tf_op jit(solution)/shard_map/ppermute | solution.py:72
  207.4 10.1 %collective-permute-done.22 = bf16[64,4096]{1,0:T(8,128)(2,1)S(1)} collective-permute-done((bf16[64,4096]{1,0:T(8,128)(2,1)S(1)}, bf16[64,4096]{1,0:T(8,128)(2,1)S(1)}, u32[]{:S(2)}, u32[]{:S(2)}) %collective-permute-start.22) | collective-permute-done | bytes 524320 | tf_op jit(solution)/shard_map/ppermute | solution.py:72
  217.5 10.3 %collective-permute-done.24 = bf16[64,4096]{1,0:T(8,128)(2,1)S(1)} collective-permute-done((bf16[64,4096]{1,0:T(8,128)(2,1)S(1)}, bf16[64,4096]{1,0:T(8,128)(2,1)S(1)}, u32[]{:S(2)}, u32[]{:S(2)}) %collective-permute-start.24) | collective-permute-done | bytes 524320 | tf_op jit(solution)/shard_map/ppermute | solution.py:72
  (103 shorter events, 30.6 us)
Async XLA Ops:
  6.5 3.3 %copy-start = (bf16[4096,256]{1,0:T(8,128)(2,1)S(1)}, bf16[4096,256]{1,0:T(8,128)(2,1)}, u32[]{:S(2)}) copy-start(bf16[4096,256]{1,0:T(8,128)(2,1)} %param.10) | copy-start | bytes 6291460
  6.5 13.9 %copy-start.11 = (s32[16]{0:T(128)S(1)}, s32[16]{0:T(128)}, u32[]{:S(2)}) copy-start(s32[16]{0:T(128)} %param.16) | copy-start | bytes 196
  6.5 16.0 %copy-start.10 = (s32[512]{0:T(512)S(1)}, s32[512]{0:T(512)}, u32[]{:S(2)}) copy-start(s32[512]{0:T(512)} %param.17) | copy-start | bytes 6148
  6.5 20.5 %copy-start.6 = (bf16[64,4096]{1,0:T(8,128)(2,1)S(1)}, bf16[64,4096]{1,0:T(8,128)(2,1)}, u32[]{:S(2)}) copy-start(bf16[64,4096]{1,0:T(8,128)(2,1)} %param.9) | copy-start | bytes 1572868
  6.5 80.7 %all-gather.4.cloned.1.call-start = ((), (), s32[]{:S(2)}) async-start(), calls=%async_computation.2 | async-start | bytes 3612672 | tf_op jit(solution)/shard_map/all_gather | solution.py:301
  10.7 19.2 %collective-permute-start = (bf16[736,256]{1,0:T(8,128)(2,1)}, bf16[736,256]{1,0:T(8,128)(2,1)}, u32[]{:S(2)}, u32[]{:S(2)}) collective-permute-start(bf16[736,256]{1,0:T(8,128)(2,1)} %pad_maximum_fusion.4), channel_id=1, source_target_pairs={{0,0},{1,1},{2,2},{3,3},{4,4},{5,5},{6,6},{7,7},{8,8},{9,9},{10,10... | collective-permute-start | bytes 1130504 | tf_op jit(solution)/shard_map/ppermute | solution.py:72
  30.0 27.2 %all-to-all-start = ((bf16[16,24,896]{2,1,0:T(8,128)(2,1)}), bf16[16,24,896]{2,1,0:T(8,128)(2,1)}, u32[]{:S(2)}, u32[]{:S(2)}) async-start(bf16[16,24,896]{2,1,0:T(8,128)(2,1)} %bitcast.5), calls=%async_computation | async-start | bytes 1376256 | tf_op jit(solution)/shard_map/all_to_all | solution.py:323
  43.9 97.6 %all-gather.8.cloned.1.call-start = ((), (), s32[]{:S(2)}) async-start(), calls=%async_computation.4 | async-start | bytes 3391488 | tf_op jit(solution)/shard_map/all_gather | solution.py:330
  44.1 24.5 %collective-permute-start.1 = (bf16[736,256]{1,0:T(8,128)(2,1)}, bf16[736,256]{1,0:T(8,128)(2,1)}, u32[]{:S(2)}, u32[]{:S(2)}) collective-permute-start(bf16[736,256]{1,0:T(8,128)(2,1)} %collective-permute-done), channel_id=1, source_target_pairs={{0,0},{1,1},{2,18},{3,19},{4,68},{5,69},{6,86},{7,87},{8,136},{9,1... | collective-permute-start | bytes 1130504 | tf_op jit(solution)/shard_map/ppermute | solution.py:72
  49.2 19.5 %collective-permute-start.2 = (bf16[512,256]{1,0:T(8,128)(2,1)}, bf16[512,256]{1,0:T(8,128)(2,1)}, u32[]{:S(2)}, u32[]{:S(2)}) collective-permute-start(bf16[512,256]{1,0:T(8,128)(2,1)} %pad_maximum_fusion.5), channel_id=1, source_target_pairs={{0,0},{1,1},{2,2},{3,3},{4,4},{5,5},{6,6},{7,7},{8,8},{9,9},{10,10... | collective-permute-start | bytes 786440 | tf_op jit(solution)/shard_map/ppermute | solution.py:72
  68.6 18.6 %all-to-all-start.1 = ((bf16[16,16,896]{2,1,0:T(8,128)(2,1)}), bf16[16,16,896]{2,1,0:T(8,128)(2,1)S(1)}, u32[]{:S(2)}, u32[]{:S(2)}) async-start(bf16[16,16,896]{2,1,0:T(8,128)(2,1)} %bitcast.6), calls=%async_computation.1 | async-start | bytes 917504 | tf_op jit(solution)/shard_map/all_to_all | solution.py:329
  72.7 116.9 %all-gather.6.cloned.1.call-start = ((), (), s32[]{:S(2)}) async-start(), calls=%async_computation.3 | async-start | bytes 4718592 | tf_op jit(solution)/shard_map/all_gather | solution.py:341
  72.8 9.0 %collective-permute-start.3 = (bf16[512,256]{1,0:T(8,128)(2,1)}, bf16[512,256]{1,0:T(8,128)(2,1)S(1)}, u32[]{:S(2)}, u32[]{:S(2)}) collective-permute-start(bf16[512,256]{1,0:T(8,128)(2,1)} %collective-permute-done.2), channel_id=1, source_target_pairs={{0,0},{1,1},{2,18},{3,19},{4,68},{5,69},{6,86},{7,87},{8,136},{9,1... | collective-permute-start | bytes 786440 | tf_op jit(solution)/shard_map/ppermute | solution.py:72
  81.8 5.5 %copy-start.9 = (bf16[512,256]{1,0:T(8,128)(2,1)}, bf16[512,256]{1,0:T(8,128)(2,1)S(1)}, u32[]{:S(2)}) copy-start(bf16[512,256]{1,0:T(8,128)(2,1)S(1)} %collective-permute-done.3) | copy-start | bytes 786436
  87.3 14.0 %collective-permute-start.5 = (bf16[1792,896]{1,0:T(8,128)(2,1)}, bf16[1792,896]{1,0:T(8,128)(2,1)S(1)}, u32[]{:S(2)}, u32[]{:S(2)}) collective-permute-start(bf16[1792,896]{1,0:T(8,128)(2,1)} %all-gather.4.cloned.1.call-done), channel_id=1, source_target_pairs={{0,16},{1,17},{2,18},{3,19},{4,20},{5,21},{6,22},{7,23},{8,24},{9,... | collective-permute-start | bytes 9633800 | tf_op jit(solution)/shard_map/ppermute | solution.py:72
  90.7 10.5 %collective-permute-start.4 = (bf16[256,896]{1,0:T(8,128)(2,1)S(1)}, bf16[256,896]{1,0:T(8,128)(2,1)S(1)}, u32[]{:S(2)}, u32[]{:S(2)}) collective-permute-start(bf16[256,896]{1,0:T(8,128)(2,1)S(1)} %bitcast.34), channel_id=1, source_target_pairs={{0,1},{1,32},{2,3},{3,34},{4,5},{5,36},{6,7},{7,38},{8,9},{9,40},{... | collective-permute-start | bytes 1376264 | tf_op jit(solution)/shard_map/ppermute | solution.py:72
  90.7 10.5 %collective-permute-start.6 = (bf16[512,256]{1,0:T(8,128)(2,1)}, bf16[512,256]{1,0:T(8,128)(2,1)S(1)}, u32[]{:S(2)}, u32[]{:S(2)}) collective-permute-start(bf16[512,256]{1,0:T(8,128)(2,1)} %copy-done.9), channel_id=1, source_target_pairs={{0,1},{1,32},{2,3},{3,34},{4,5},{5,36},{6,7},{7,38},{8,9},{9,40},{... | collective-permute-start | bytes 786440 | tf_op jit(solution)/shard_map/ppermute | solution.py:72
  101.3 1.8 copy-start.4
  104.9 1.9 copy-start.3
  106.8 1.9 copy-start.5
  113.7 11.3 %collective-permute-start.7 = (bf16[256,896]{1,0:T(8,128)(2,1)S(1)}, bf16[256,896]{1,0:T(8,128)(2,1)S(1)}, u32[]{:S(2)}, u32[]{:S(2)}) collective-permute-start(bf16[256,896]{1,0:T(8,128)(2,1)S(1)} %encode.2), channel_id=1, source_target_pairs={{0,33},{1,0},{2,35},{3,2},{4,37},{5,4},{6,39},{7,6},{8,41},{9,8},{... | collective-permute-start | bytes 1376264 | tf_op jit(solution)/shard_map/ppermute | solution.py:72
  114.2 13.0 %collective-permute-start.10 = (bf16[64,4096]{1,0:T(8,128)(2,1)S(1)}, bf16[64,4096]{1,0:T(8,128)(2,1)}, u32[]{:S(2)}, u32[]{:S(2)}) collective-permute-start(bf16[64,4096]{1,0:T(8,128)(2,1)S(1)} %fusion.2), channel_id=1, source_target_pairs={{0,192},{1,193},{2,194},{3,195},{4,196},{5,197},{6,198},{7,199},{8... | collective-permute-start | bytes 1572872 | tf_op jit(solution)/shard_map/ppermute | solution.py:72
  117.0 13.0 %collective-permute-start.8 = (bf16[64,4096]{1,0:T(8,128)(2,1)S(1)}, bf16[64,4096]{1,0:T(8,128)(2,1)}, u32[]{:S(2)}, u32[]{:S(2)}) collective-permute-start(bf16[64,4096]{1,0:T(8,128)(2,1)S(1)} %fusion.2), channel_id=1, source_target_pairs={{0,64},{1,65},{2,66},{3,67},{4,68},{5,69},{6,70},{7,71},{8,72},{9,... | collective-permute-start | bytes 1572872 | tf_op jit(solution)/shard_map/ppermute | solution.py:72
  117.0 24.6 %collective-permute-start.9 = (bf16[64,4096]{1,0:T(8,128)(2,1)S(1)}, bf16[64,4096]{1,0:T(8,128)(2,1)}, u32[]{:S(2)}, u32[]{:S(2)}) collective-permute-start(bf16[64,4096]{1,0:T(8,128)(2,1)S(1)} %fusion.2), channel_id=1, source_target_pairs={{0,128},{1,129},{2,130},{3,131},{4,132},{5,133},{6,134},{7,135},{8... | collective-permute-start | bytes 1572872 | tf_op jit(solution)/shard_map/ppermute | solution.py:72
  141.5 4.6 %copy-start.8 = (bf16[5888,256]{1,0:T(8,128)(2,1)S(1)}, bf16[5888,256]{1,0:T(8,128)(2,1)}, u32[]{:S(2)}) copy-start(bf16[5888,256]{1,0:T(8,128)(2,1)} %all-gather.8.cloned.1.call-done) | copy-start | bytes 9043972
  143.3 27.8 %collective-permute-start.12 = (bf16[256,4096]{1,0:T(8,128)(2,1)S(1)}, bf16[256,4096]{1,0:T(8,128)(2,1)S(1)}, u32[]{:S(2)}, u32[]{:S(2)}) collective-permute-start(bf16[256,4096]{1,0:T(8,128)(2,1)S(1)} %pad_maximum_fusion), channel_id=1, source_target_pairs={{0,16},{1,17},{2,18},{3,19},{4,20},{5,21},{6,22},{7,23},{8,24},{9,... | collective-permute-start | bytes 6291464 | tf_op jit(solution)/shard_map/ppermute | solution.py:72
  146.3 11.9 %collective-permute-start.18 = (bf16[256,896]{1,0:T(8,128)(2,1)S(1)}, bf16[256,896]{1,0:T(8,128)(2,1)S(1)}, u32[]{:S(2)}, u32[]{:S(2)}) collective-permute-start(bf16[256,896]{1,0:T(8,128)(2,1)S(1)} %add_convert_fusion.3.refs_1_), channel_id=1, source_target_pairs={{0,192},{1,193},{2,194},{3,195},{4,196},{5,197},{6,198},{7,199},{8... | collective-permute-start | bytes 1376264 | tf_op jit(solution)/shard_map/ppermute | solution.py:72
  146.6 13.4 %collective-permute-start.16 = (bf16[256,896]{1,0:T(8,128)(2,1)S(1)}, bf16[256,896]{1,0:T(8,128)(2,1)S(1)}, u32[]{:S(2)}, u32[]{:S(2)}) collective-permute-start(bf16[256,896]{1,0:T(8,128)(2,1)S(1)} %add_convert_fusion.3.refs_1_), channel_id=1, source_target_pairs={{0,128},{1,129},{2,130},{3,131},{4,132},{5,133},{6,134},{7,135},{8... | collective-permute-start | bytes 1376264 | tf_op jit(solution)/shard_map/ppermute | solution.py:72
  147.7 22.8 %collective-permute-start.14 = (bf16[256,896]{1,0:T(8,128)(2,1)S(1)}, bf16[256,896]{1,0:T(8,128)(2,1)S(1)}, u32[]{:S(2)}, u32[]{:S(2)}) collective-permute-start(bf16[256,896]{1,0:T(8,128)(2,1)S(1)} %add_convert_fusion.3.refs_1_), channel_id=1, source_target_pairs={{0,64},{1,65},{2,66},{3,67},{4,68},{5,69},{6,70},{7,71},{8,72},{9,... | collective-permute-start | bytes 1376264 | tf_op jit(solution)/shard_map/ppermute | solution.py:72
  148.0 31.6 %collective-permute-start.11 = (bf16[4096,256]{1,0:T(8,128)(2,1)S(1)}, bf16[4096,256]{1,0:T(8,128)(2,1)S(1)}, u32[]{:S(2)}, u32[]{:S(2)}) collective-permute-start(bf16[4096,256]{1,0:T(8,128)(2,1)S(1)} %bitcast.32), channel_id=1, source_target_pairs={{0,1},{1,32},{2,3},{3,34},{4,5},{5,36},{6,7},{7,38},{8,9},{9,40},{... | collective-permute-start | bytes 6291464 | tf_op jit(solution)/shard_map/ppermute | solution.py:72
  158.2 24.9 %collective-permute-start.20 = (bf16[1792,256]{1,0:T(8,128)(2,1)S(1)}, bf16[1792,256]{1,0:T(8,128)(2,1)S(1)}, u32[]{:S(2)}, u32[]{:S(2)}) collective-permute-start(bf16[1792,256]{1,0:T(8,128)(2,1)S(1)} %pad_maximum_fusion.1.refs_3_), channel_id=1, source_target_pairs={{0,1},{1,32},{2,3},{3,34},{4,5},{5,36},{6,7},{7,38},{8,9},{9,40},{... | collective-permute-start | bytes 2752520 | tf_op jit(solution)/shard_map/ppermute | solution.py:72
  160.0 10.9 %collective-permute-start.19 = (bf16[256,896]{1,0:T(8,128)(2,1)S(1)}, bf16[256,896]{1,0:T(8,128)(2,1)S(1)}, u32[]{:S(2)}, u32[]{:S(2)}) collective-permute-start(bf16[256,896]{1,0:T(8,128)(2,1)S(1)} %collective-permute-done.18.refs_1_), channel_id=1, source_target_pairs={{0,16},{1,17},{2,18},{3,19},{4,20},{5,21},{6,22},{7,23},{8,24},{9,... | collective-permute-start | bytes 1376264 | tf_op jit(solution)/shard_map/ppermute | solution.py:72
  170.5 7.4 %collective-permute-start.13 = (bf16[256,896]{1,0:T(8,128)(2,1)S(1)}, bf16[256,896]{1,0:T(8,128)(2,1)S(1)}, u32[]{:S(2)}, u32[]{:S(2)}) collective-permute-start(bf16[256,896]{1,0:T(8,128)(2,1)S(1)} %add_convert_fusion.3.refs_1_), channel_id=1, source_target_pairs={{0,16},{1,17},{2,18},{3,19},{4,20},{5,21},{6,22},{7,23},{8,24},{9,... | collective-permute-start | bytes 1376264 | tf_op jit(solution)/shard_map/ppermute | solution.py:72
  170.9 3.7 %collective-permute-start.17 = (bf16[256,896]{1,0:T(8,128)(2,1)S(1)}, bf16[256,896]{1,0:T(8,128)(2,1)S(1)}, u32[]{:S(2)}, u32[]{:S(2)}) collective-permute-start(bf16[256,896]{1,0:T(8,128)(2,1)S(1)} %collective-permute-done.16.refs_1_), channel_id=1, source_target_pairs={{0,16},{1,17},{2,18},{3,19},{4,20},{5,21},{6,22},{7,23},{8,24},{9,... | collective-permute-start | bytes 1376264 | tf_op jit(solution)/shard_map/ppermute | solution.py:72
  171.0 5.2 %collective-permute-start.15 = (bf16[256,896]{1,0:T(8,128)(2,1)S(1)}, bf16[256,896]{1,0:T(8,128)(2,1)S(1)}, u32[]{:S(2)}, u32[]{:S(2)}) collective-permute-start(bf16[256,896]{1,0:T(8,128)(2,1)S(1)} %collective-permute-done.14.refs_1_), channel_id=1, source_target_pairs={{0,16},{1,17},{2,18},{3,19},{4,20},{5,21},{6,22},{7,23},{8,24},{9,... | collective-permute-start | bytes 1376264 | tf_op jit(solution)/shard_map/ppermute | solution.py:72
  189.7 2.2 copy-start.1
  193.2 6.6 %copy-start.2 = (bf16[8192,256]{1,0:T(8,128)(2,1)S(1)}, bf16[8192,256]{1,0:T(8,128)(2,1)}, u32[]{:S(2)}) copy-start(bf16[8192,256]{1,0:T(8,128)(2,1)} %all-gather.6.cloned.1.call-done) | copy-start | bytes 12582916
  193.2 8.1 %collective-permute-start.21 = (bf16[64,4096]{1,0:T(8,128)(2,1)S(1)}, bf16[64,4096]{1,0:T(8,128)(2,1)S(1)}, u32[]{:S(2)}, u32[]{:S(2)}) collective-permute-start(bf16[64,4096]{1,0:T(8,128)(2,1)S(1)} %get-tuple-element.82), channel_id=1, source_target_pairs={{0,16},{1,17},{2,18},{3,19},{4,20},{5,21},{6,22},{7,23},{8,24},{9,... | collective-permute-start | bytes 1572872 | tf_op jit(solution)/shard_map/ppermute | solution.py:72
  197.8 7.8 %collective-permute-start.23 = (bf16[64,4096]{1,0:T(8,128)(2,1)S(1)}, bf16[64,4096]{1,0:T(8,128)(2,1)S(1)}, u32[]{:S(2)}, u32[]{:S(2)}) collective-permute-start(bf16[64,4096]{1,0:T(8,128)(2,1)S(1)} %get-tuple-element.86), channel_id=1, source_target_pairs={{0,16},{1,17},{2,18},{3,19},{4,20},{5,21},{6,22},{7,23},{8,24},{9,... | collective-permute-start | bytes 1572872 | tf_op jit(solution)/shard_map/ppermute | solution.py:72
  199.3 6.5 %collective-permute-start.25 = (bf16[64,4096]{1,0:T(8,128)(2,1)S(1)}, bf16[64,4096]{1,0:T(8,128)(2,1)S(1)}, u32[]{:S(2)}, u32[]{:S(2)}) collective-permute-start(bf16[64,4096]{1,0:T(8,128)(2,1)S(1)} %get-tuple-element.90), channel_id=1, source_target_pairs={{0,16},{1,17},{2,18},{3,19},{4,20},{5,21},{6,22},{7,23},{8,24},{9,... | collective-permute-start | bytes 1572872 | tf_op jit(solution)/shard_map/ppermute | solution.py:72
  201.2 28.1 %copy-start.7 = (bf16[64,4096]{1,0:T(8,128)(2,1)S(1)}, bf16[64,4096]{1,0:T(8,128)(2,1)}, u32[]{:S(2)}) copy-start(bf16[64,4096]{1,0:T(8,128)(2,1)} %param.9) | copy-start | bytes 1572868
  201.2 6.2 %collective-permute-start.27 = (bf16[64,4096]{1,0:T(8,128)(2,1)S(1)}, bf16[64,4096]{1,0:T(8,128)(2,1)S(1)}, u32[]{:S(2)}, u32[]{:S(2)}) collective-permute-start(bf16[64,4096]{1,0:T(8,128)(2,1)S(1)} %get-tuple-element.94), channel_id=1, source_target_pairs={{0,16},{1,17},{2,18},{3,19},{4,20},{5,21},{6,22},{7,23},{8,24},{9,... | collective-permute-start | bytes 1572872 | tf_op jit(solution)/shard_map/ppermute | solution.py:72
  201.4 16.1 %collective-permute-start.22 = (bf16[64,4096]{1,0:T(8,128)(2,1)S(1)}, bf16[64,4096]{1,0:T(8,128)(2,1)S(1)}, u32[]{:S(2)}, u32[]{:S(2)}) collective-permute-start(bf16[64,4096]{1,0:T(8,128)(2,1)S(1)} %add_convert_fusion.2), channel_id=1, source_target_pairs={{0,128},{1,129},{2,130},{3,131},{4,132},{5,133},{6,134},{7,135},{8... | collective-permute-start | bytes 1572872 | tf_op jit(solution)/shard_map/ppermute | solution.py:72
  205.7 22.1 %collective-permute-start.24 = (bf16[64,4096]{1,0:T(8,128)(2,1)S(1)}, bf16[64,4096]{1,0:T(8,128)(2,1)S(1)}, u32[]{:S(2)}, u32[]{:S(2)}) collective-permute-start(bf16[64,4096]{1,0:T(8,128)(2,1)S(1)} %add_convert_fusion.1), channel_id=1, source_target_pairs={{0,192},{1,193},{2,194},{3,195},{4,196},{5,197},{6,198},{7,199},{8... | collective-permute-start | bytes 1572872 | tf_op jit(solution)/shard_map/ppermute | solution.py:72
  205.9 23.3 %collective-permute-start.26 = (bf16[64,4096]{1,0:T(8,128)(2,1)S(1)}, bf16[64,4096]{1,0:T(8,128)(2,1)S(1)}, u32[]{:S(2)}, u32[]{:S(2)}) collective-permute-start(bf16[64,4096]{1,0:T(8,128)(2,1)S(1)} %add_convert_fusion), channel_id=1, source_target_pairs={{0,64},{1,65},{2,66},{3,67},{4,68},{5,69},{6,70},{7,71},{8,72},{9,... | collective-permute-start | bytes 1572872 | tf_op jit(solution)/shard_map/ppermute | solution.py:72
Sparse Core Ops, SparseCore 0:
  9.2 55.0 all-gather.3
  68.8 45.7 all-gather.7
  116.4 54.6 all-gather.5

commit v3 on v1

--- a/solution.py
+++ b/solution.py
@@ -236,43 +236,46 @@
     )(q, enc_0, enc_1, kv)
 
 
-def project_kernel(mixed_a, mixed_b, weight, near, far):
-    half = mixed_a.shape[1]
+def project_kernel(count, *refs):
+    mixed, (weight, near, far) = refs[: 2 * count], refs[2 * count :]
+    sides = [
+        jnp.concatenate(
+            [m[i * CT : (i + 1) * CT] for i in range(2) for m in half], axis=0
+        )
+        for half in (mixed[:count], mixed[count:])
+    ]
     width = weight.shape[3]
+    blocks = weight.shape[1] // 2
     for plane in range(weight.shape[0]):
-        for block in range(weight.shape[1] // 2):
-            start = (plane * weight.shape[1] // 2 + block) * width
-            out = matmul(mixed_a[...], weight[plane, block])
-            out = out + matmul(mixed_b[...], weight[plane, weight.shape[1] // 2 + block])
-            near[:, start : start + width] = out[:CT]
-            far[:, start : start + width] = out[CT:].astype(jnp.bfloat16)
-
-
-def project(mixed_a, mixed_b, weight):
-    count, half = mixed_a.shape
+        for block in range(blocks):
+            start = (plane * blocks + block) * width
+            out = matmul(sides[0], weight[plane, block])
+            out = out + matmul(sides[1], weight[plane, blocks + block])
+            near[:, start : start + width] = out[: count * CT]
+            far[:, start : start + width] = out[count * CT :].astype(jnp.bfloat16)
+
+
+def project(mixed, weight):
+    count = len(mixed) // 2
+    half = mixed[0].shape[1]
     planes, steps = 8, 4
     weight = weight.reshape(planes, -1, half, weight.shape[1])
-    blocks = weight.shape[1]
-    width = planes * blocks // 2 * weight.shape[3]
-    rows = pl.BlockSpec((count, half), lambda i: (0, 0))
-    out = pl.BlockSpec((CT, width // steps), lambda i: (0, i))
+    width = planes * weight.shape[1] // 2 * weight.shape[3]
+    out = pl.BlockSpec((count * CT, width // steps), lambda i: (0, i))
     return pl.pallas_call(
-        project_kernel,
+        lambda *refs: project_kernel(count, *refs),
         grid=(steps,),
-        in_specs=[
-            rows,
-            rows,
-            pl.BlockSpec((planes // steps,) + weight.shape[1:], lambda i: (i, 0, 0, 0)),
-        ],
+        in_specs=[pl.BlockSpec(m.shape, lambda i: (0, 0)) for m in mixed]
+        + [pl.BlockSpec((planes // steps,) + weight.shape[1:], lambda i: (i, 0, 0, 0))],
         out_specs=[out, out],
         out_shape=[
-            jax.ShapeDtypeStruct((CT, width), jnp.float32),
-            jax.ShapeDtypeStruct((CT, width), jnp.bfloat16),
+            jax.ShapeDtypeStruct((count * CT, width), jnp.float32),
+            jax.ShapeDtypeStruct((count * CT, width), jnp.bfloat16),
         ],
-        compiler_params=pltpu.CompilerParams(vmem_limit_bytes=32 * 2**20),
+        compiler_params=pltpu.CompilerParams(vmem_limit_bytes=40 * 2**20),
         cost_estimate=pl.CostEstimate(flops=1, bytes_accessed=1, transcendentals=0),
         name="project",
-    )(mixed_a, mixed_b, weight)
+    )(*mixed, weight)
 
 
 def together(*values):
@@ -317,6 +320,7 @@
     normed = rms_normed(hidden_states)
 
     packed, placing = pack(neighbours, counts, slot_of)
+    packed, normed = together(packed, normed)
     arrived = lax.all_to_all(packed, ("y", "xh", "core"), split_axis=0, concat_axis=0, tiled=True)
     in_piece = send(in_piece, along_z(steps_a))
     token_1, token_3 = send(normed, Y_UP[1]), send(normed, Y_UP[3])
@@ -371,13 +375,15 @@
     mixed_b = mix(query(tokens, q_b), kv_b)
 
     out_weight, *mixed = together(out_weight, *mixed_a, *mixed_b)
+    near, far = project(mixed, out_weight)
+    far = send(far, CORE)
     total = hidden_states.astype(jnp.float32)
     for d in (2, 1, 3, 0):
-        near, far = project(mixed[d], mixed[4 + d], out_weight)
-        near = near + send(far, CORE).astype(jnp.float32)
+        rows = slice(d * CT, (d + 1) * CT)
+        summed = near[rows] + far[rows].astype(jnp.float32)
         if d:
-            near = send(near.astype(jnp.bfloat16), Y_UP[4 - d]).astype(jnp.float32)
-        total = total + near
+            summed = send(summed.astype(jnp.bfloat16), Y_UP[4 - d]).astype(jnp.float32)
+        total = total + summed
     return total.astype(jnp.bfloat16)
 
 

time: 224 us -> 224 us (level)
  starting transfers between devices: 69.5 us -> 74.3 us
    ppermute x28 -> x25, starting transfers between devices: 55.3 us -> 59.6 us  [send(): return lax.ppermute(x, AXES, perm)]
    pallas_call x4 -> x1, Pallas kernels: 5.3 us -> 3.24 us  [project(): pl.pallas_call(lambda *refs: project_kernel(count, *refs), grid=(steps,),...]
    ppermute x28 -> x25, waiting for transfers between devices: 61.2 us -> 59.7 us  [send(): return lax.ppermute(x, AXES, perm)]
  transfers between devices with their start and end apart: 33 -> 30, of which waited for: 15 -> 17; matrix products, arithmetic and copies ran while one was open for 10% -> 9% of each run, Pallas kernels for 14% -> 12%
where the time goes in v3:
time: 224 us; the launch traced here: 223 us
  waiting for transfers between devices  78.1 us (35%)
  starting transfers between devices  74.3 us (33%)
  Pallas kernels  29.7 us (13%)
  local copies, waits for them, and re-layouts  15.3 us (7%)
  between operations  13.5 us (6%)
  other arithmetic  10.3 us (5%)
    ppermute x25, waiting for transfers between devices, send(): return lax.ppermute(x, AXES, perm)  59.7 us
    ppermute x25, starting transfers between devices, send(): return lax.ppermute(x, AXES, perm)  59.6 us
    pallas_call x8, Pallas kernels, attend(): pl.pallas_call(lambda *refs: attend_kernel(first, *refs), out_shape=jax.S...  13.2 us
    pallas_call x2, Pallas kernels, encode(): pl.pallas_call(lambda *refs: encode_kernel(steps, keep_raw, *refs), grid=...  10.8 us
    unnamed x20, local copies, waits for them, and re-layouts  8.48 us
    all_to_all x1, starting transfers between devices, body(): lax.all_to_all(placed, ('z', 'xl'), split_axis=0, concat_axis=0, tiled=True)  7.69 us
    all_to_all x1, waiting for transfers between devices, body(): lax.all_to_all(placed, ('z', 'xl'), split_axis=0, concat_axis=0, tiled=True)  6.98 us
    all_to_all x1, starting transfers between devices, body(): lax.all_to_all(packed, ('y', 'xh', 'core'), split_axis=0, concat_axis=0,...  6.9 us
  transfers between devices with their start and end apart: 30, of which 17 were waited for; matrix products, arithmetic and copies ran while one was open for 9% of the time, Pallas kernels for 12%

profile of v3, /device:TPU:1, one launch (start us, length us, event | category | flops | bytes accessed | tf_op | source)
XLA Modules:
  0.0 223.3 jit_solution(2152146081438154728)
XLA Ops:
  6.5 1.2 constant_dynamic-slice_fusion.1
  11.3 1.6 convolution_convert_fusion.1
  15.1 2.1 collective-permute-start.1
  17.2 1.4 collective-permute-start.2
  18.6 6.9 %all-to-all-start = ((bf16[16,24,896]{2,1,0:T(8,128)(2,1)}), bf16[16,24,896]{2,1,0:T(8,128)(2,1)S(1)}, u32[]{:S(2)}, u32[]{:S(2)}) async-start(bf16[16,24,896]{2,1,0:T(8,128)(2,1)} %bitcast.3), calls=%async_computation | async-start | bytes 1376256 | tf_op jit(solution)/shard_map/all_to_all | solution.py:324
  25.6 1.2 constant_dynamic-slice_fusion
  27.6 8.8 %collective-permute-start = (bf16[736,256]{1,0:T(8,128)(2,1)}, bf16[736,256]{1,0:T(8,128)(2,1)}, u32[]{:S(2)}, u32[]{:S(2)}) collective-permute-start(bf16[736,256]{1,0:T(8,128)(2,1)} %pad_maximum_fusion.4), channel_id=1, source_target_pairs={{0,0},{1,1},{2,2},{3,3},{4,4},{5,5},{6,6},{7,7},{8,8},{9,9},{10,10... | collective-permute-start | bytes 1130504 | tf_op jit(solution)/shard_map/ppermute | solution.py:72
  36.4 3.2 %all-to-all-done = bf16[16,24,896]{2,1,0:T(8,128)(2,1)S(1)} async-done(((bf16[16,24,896]{2,1,0:T(8,128)(2,1)}), bf16[16,24,896]{2,1,0:T(8,128)(2,1)S(1)}, u32[]{:S(2)}, u32[]{:S(2)}) %all-to-all-start) | async-done | bytes 688160 | tf_op jit(solution)/shard_map/all_to_all | solution.py:324
  41.4 11.2 %collective-permute-done = bf16[736,256]{1,0:T(8,128)(2,1)} collective-permute-done((bf16[736,256]{1,0:T(8,128)(2,1)}, bf16[736,256]{1,0:T(8,128)(2,1)}, u32[]{:S(2)}, u32[]{:S(2)}) %collective-permute-start) | collective-permute-done | bytes 376864 | tf_op jit(solution)/shard_map/ppermute | solution.py:72
  52.5 7.7 %all-to-all-start.1 = ((bf16[16,16,896]{2,1,0:T(8,128)(2,1)}), bf16[16,16,896]{2,1,0:T(8,128)(2,1)S(1)}, u32[]{:S(2)}, u32[]{:S(2)}) async-start(bf16[16,16,896]{2,1,0:T(8,128)(2,1)} %bitcast.6), calls=%async_computation.1 | async-start | bytes 917504 | tf_op jit(solution)/shard_map/all_to_all | solution.py:330
  60.3 4.5 %collective-permute-start.3 = (bf16[736,256]{1,0:T(8,128)(2,1)}, bf16[736,256]{1,0:T(8,128)(2,1)S(1)}, u32[]{:S(2)}, u32[]{:S(2)}) collective-permute-start(bf16[736,256]{1,0:T(8,128)(2,1)} %collective-permute-done), channel_id=1, source_target_pairs={{0,0},{1,1},{2,18},{3,19},{4,68},{5,69},{6,86},{7,87},{8,136},{9,1... | collective-permute-start | bytes 1130504 | tf_op jit(solution)/shard_map/ppermute | solution.py:72
  65.9 3.8 %collective-permute-done.3 = bf16[736,256]{1,0:T(8,128)(2,1)S(1)} collective-permute-done((bf16[736,256]{1,0:T(8,128)(2,1)}, bf16[736,256]{1,0:T(8,128)(2,1)S(1)}, u32[]{:S(2)}, u32[]{:S(2)}) %collective-permute-start.3) | collective-permute-done | bytes 376864 | tf_op jit(solution)/shard_map/ppermute | solution.py:72
  69.7 7.0 %all-to-all-done.1 = bf16[16,16,896]{2,1,0:T(8,128)(2,1)S(1)} async-done(((bf16[16,16,896]{2,1,0:T(8,128)(2,1)}), bf16[16,16,896]{2,1,0:T(8,128)(2,1)S(1)}, u32[]{:S(2)}, u32[]{:S(2)}) %all-to-all-start.1) | async-done | bytes 458784 | tf_op jit(solution)/shard_map/all_to_all | solution.py:330
  77.3 2.1 collective-permute-start.4
  79.5 6.8 %collective-permute-start.6 = (bf16[512,256]{1,0:T(8,128)(2,1)S(1)}, bf16[512,256]{1,0:T(8,128)(2,1)S(1)}, u32[]{:S(2)}, u32[]{:S(2)}) collective-permute-start(bf16[512,256]{1,0:T(8,128)(2,1)S(1)} %pad_maximum_fusion.5), channel_id=1, source_target_pairs={{0,0},{1,1},{2,2},{3,3},{4,4},{5,5},{6,6},{7,7},{8,8},{9,9},{10,10... | collective-permute-start | bytes 786440 | tf_op jit(solution)/shard_map/ppermute | solution.py:72
  86.3 4.3 %collective-permute-done.6 = bf16[512,256]{1,0:T(8,128)(2,1)S(1)} collective-permute-done((bf16[512,256]{1,0:T(8,128)(2,1)S(1)}, bf16[512,256]{1,0:T(8,128)(2,1)S(1)}, u32[]{:S(2)}, u32[]{:S(2)}) %collective-permute-start.6) | collective-permute-done | bytes 262176 | tf_op jit(solution)/shard_map/ppermute | solution.py:72
  90.6 7.4 %collective-permute-start.7 = (bf16[512,256]{1,0:T(8,128)(2,1)S(1)}, bf16[512,256]{1,0:T(8,128)(2,1)S(1)}, u32[]{:S(2)}, u32[]{:S(2)}) collective-permute-start(bf16[512,256]{1,0:T(8,128)(2,1)S(1)} %collective-permute-done.6), channel_id=1, source_target_pairs={{0,0},{1,1},{2,18},{3,19},{4,68},{5,69},{6,86},{7,87},{8,136},{9,1... | collective-permute-start | bytes 786440 | tf_op jit(solution)/shard_map/ppermute | solution.py:72
  98.0 1.9 copy-done.1
  100.0 5.7 %encode.2 = bf16[256,896]{1,0:T(8,128)(2,1)} custom-call(bf16[256,896]{1,0:T(8,128)(2,1)S(1)} %collective-permute-done.4.refs_0_, bf16[16,112,896]{2,1,0:T(8,128)(2,1)S(1)} %bitcast.24, bf16[16,112,896]{2,1,0:T(8,128)(2,1)S(1)} %bitcast.26), custom_call_target="tpu_custom_call" | custom-call | flops 1 | bytes 1 | tf_op jit(solution)/shard_map/encode/pallas_call | solution.py:182
  105.7 1.7 collective-permute-start.8
  108.4 5.0 %encode.3 = f32[256,896]{1,0:T(8,128)S(1)} custom-call(bf16[256,896]{1,0:T(8,128)(2,1)S(1)} %bitcast.32, bf16[16,112,896]{2,1,0:T(8,128)(2,1)S(1)} %bitcast.25, bf16[16,112,896]{2,1,0:T(8,128)(2,1)S(1)} %bitcast.27), custom_call_target="tpu_custom_call" | custom-call | flops 1 | bytes 1 | tf_op jit(solution)/shard_map/encode/pallas_call | solution.py:182
  115.9 6.8 %collective-permute-done.9 = bf16[64,4096]{1,0:T(8,128)(2,1)} collective-permute-done((bf16[64,4096]{1,0:T(8,128)(2,1)}, bf16[64,4096]{1,0:T(8,128)(2,1)}, u32[]{:S(2)}, u32[]{:S(2)}) %collective-permute-start.9) | collective-permute-done | bytes 524320 | tf_op jit(solution)/shard_map/ppermute | solution.py:72
  122.8 1.9 all-gather.6.cloned.1.call-done
  124.7 1.9 pad_maximum_fusion
  127.9 1.2 collective-permute-start.18
  130.3 2.4 %collective-permute-start.11 = (bf16[4096,256]{1,0:T(8,128)(2,1)S(1)}, bf16[4096,256]{1,0:T(8,128)(2,1)S(1)}, u32[]{:S(2)}, u32[]{:S(2)}) collective-permute-start(bf16[4096,256]{1,0:T(8,128)(2,1)S(1)} %bitcast.28), channel_id=1, source_target_pairs={{0,1},{1,32},{2,3},{3,34},{4,5},{5,36},{6,7},{7,38},{8,9},{9,40},{... | collective-permute-start | bytes 6291464 | tf_op jit(solution)/shard_map/ppermute | solution.py:72
  136.0 3.8 %collective-permute-done.18.refs_1_ = bf16[256,896]{1,0:T(8,128)(2,1)S(1)} collective-permute-done((bf16[256,896]{1,0:T(8,128)(2,1)S(1)}, bf16[256,896]{1,0:T(8,128)(2,1)S(1)}, u32[]{:S(2)}, u32[]{:S(2)}) %collective-permute-start.18) | collective-permute-done | bytes 458784 | tf_op jit(solution)/shard_map/ppermute | solution.py:72
  139.8 1.9 collective-permute-start.20
  141.8 9.2 %collective-permute-start.19 = (bf16[256,896]{1,0:T(8,128)(2,1)S(1)}, bf16[256,896]{1,0:T(8,128)(2,1)S(1)}, u32[]{:S(2)}, u32[]{:S(2)}) collective-permute-start(bf16[256,896]{1,0:T(8,128)(2,1)S(1)} %collective-permute-done.18.refs_1_), channel_id=1, source_target_pairs={{0,16},{1,17},{2,18},{3,19},{4,20},{5,21},{6,22},{7,23},{8,24},{9,... | collective-permute-start | bytes 1376264 | tf_op jit(solution)/shard_map/ppermute | solution.py:72
  154.0 1.3 query.2.refs_0_
  155.3 1.7 attend.11.refs_3_
  157.0 1.7 attend.10.refs_2_
  158.6 1.6 attend.9.refs_1_
  160.3 1.7 attend.8.refs_0_
  162.0 1.3 query.3.refs_0_
  163.2 2.3 %collective-permute-done.20.refs_3_ = bf16[1792,256]{1,0:T(8,128)(2,1)S(1)} collective-permute-done((bf16[1792,256]{1,0:T(8,128)(2,1)S(1)}, bf16[1792,256]{1,0:T(8,128)(2,1)S(1)}, u32[]{:S(2)}, u32[]{:S(2)}) %collective-permute-start.20) | collective-permute-done | bytes 917536 | tf_op jit(solution)/shard_map/ppermute | solution.py:72
  165.5 1.6 attend.15.refs_7_
  167.2 1.6 attend.14.refs_6_
  168.8 1.7 attend.13.refs_5_
  170.5 1.7 attend.12.refs_4_
  172.1 6.4 %all-gather.8.cloned.1.call-done = bf16[8192,256]{1,0:T(8,128)(2,1)} async-done(((bf16[1024,256]{1,0:T(8,128)(2,1)}), bf16[8192,256]{1,0:T(8,128)(2,1)}) %all-gather.8.cloned.1.call-update) | async-done | bytes 4194320 | tf_op jit(solution)/shard_map/all_gather | solution.py:353
  178.5 2.2 copy-done.2
  180.7 3.2 %project.1 = (f32[256,4096]{1,0:T(8,128)S(1)}, bf16[256,4096]{1,0:T(8,128)(2,1)S(1)}) custom-call(bf16[128,256]{1,0:T(8,128)(2,1)S(1)} %attend.8.refs_0_, bf16[128,256]{1,0:T(8,128)(2,1)S(1)} %attend.9.refs_1_, bf16[128,256]{1,0:T(8,128)(2,1)S(1)} %attend.10.refs_2_, bf16[128,256]{1,0:T(8,128)(2,1)S(1)} %attend.11.refs_3_, ...), custom_call_target="tpu_custom_call" | custom-call | flops 1 | bytes 1 | tf_op jit(solution)/shard_map/project/pallas_call | solution.py:265
  184.7 3.8 %collective-permute-done.21 = bf16[256,4096]{1,0:T(8,128)(2,1)S(1)} collective-permute-done((bf16[256,4096]{1,0:T(8,128)(2,1)S(1)}, bf16[256,4096]{1,0:T(8,128)(2,1)S(1)}, u32[]{:S(2)}, u32[]{:S(2)}) %collective-permute-start.21) | collective-permute-done | bytes 2097184 | tf_op jit(solution)/shard_map/ppermute | solution.py:72
  188.9 2.8 %collective-permute-start.22 = (bf16[64,4096]{1,0:T(8,128)(2,1)S(1)}, bf16[64,4096]{1,0:T(8,128)(2,1)S(1)}, u32[]{:S(2)}, u32[]{:S(2)}) collective-permute-start(bf16[64,4096]{1,0:T(8,128)(2,1)S(1)} %get-tuple-element.87), channel_id=1, source_target_pairs={{0,128},{1,129},{2,130},{3,131},{4,132},{5,133},{6,134},{7,135},{8... | collective-permute-start | bytes 1572872 | tf_op jit(solution)/shard_map/ppermute | solution.py:72
  193.2 10.5 %collective-permute-done.22 = bf16[64,4096]{1,0:T(8,128)(2,1)S(1)} collective-permute-done((bf16[64,4096]{1,0:T(8,128)(2,1)S(1)}, bf16[64,4096]{1,0:T(8,128)(2,1)S(1)}, u32[]{:S(2)}, u32[]{:S(2)}) %collective-permute-start.22) | collective-permute-done | bytes 524320 | tf_op jit(solution)/shard_map/ppermute | solution.py:72
  203.7 11.3 %collective-permute-done.23 = bf16[64,4096]{1,0:T(8,128)(2,1)S(1)} collective-permute-done((bf16[64,4096]{1,0:T(8,128)(2,1)S(1)}, bf16[64,4096]{1,0:T(8,128)(2,1)S(1)}, u32[]{:S(2)}, u32[]{:S(2)}) %collective-permute-start.23) | collective-permute-done | bytes 524320 | tf_op jit(solution)/shard_map/ppermute | solution.py:72
  215.6 1.2 fusion.6
  (84 shorter events, 25.7 us)
Async XLA Ops:
  6.5 19.0 %copy-start = (bf16[4096,256]{1,0:T(8,128)(2,1)S(1)}, bf16[4096,256]{1,0:T(8,128)(2,1)}, u32[]{:S(2)}) copy-start(bf16[4096,256]{1,0:T(8,128)(2,1)} %param.10) | copy-start | bytes 6291460
  6.5 7.4 %copy-start.3 = (bf16[64,4096]{1,0:T(8,128)(2,1)S(1)}, bf16[64,4096]{1,0:T(8,128)(2,1)}, u32[]{:S(2)}) copy-start(bf16[64,4096]{1,0:T(8,128)(2,1)} %param.9) | copy-start | bytes 1572868
  6.5 70.1 %all-gather.4.cloned.1.call-start = ((), (), s32[]{:S(2)}) async-start(), calls=%async_computation.2 | async-start | bytes 3612672 | tf_op jit(solution)/shard_map/all_gather | solution.py:304
  8.5 27.8 %copy-start.7 = (s32[512]{0:T(512)S(1)}, s32[512]{0:T(512)}, u32[]{:S(2)}) copy-start(s32[512]{0:T(512)} %param.17) | copy-start | bytes 6148
  15.1 37.5 %collective-permute-start.1 = (bf16[64,4096]{1,0:T(8,128)(2,1)}, bf16[64,4096]{1,0:T(8,128)(2,1)}, u32[]{:S(2)}, u32[]{:S(2)}) collective-permute-start(bf16[64,4096]{1,0:T(8,128)(2,1)} %fusion.2), channel_id=1, source_target_pairs={{0,64},{1,65},{2,66},{3,67},{4,68},{5,69},{6,70},{7,71},{8,72},{9,... | collective-permute-start | bytes 1572872 | tf_op jit(solution)/shard_map/ppermute | solution.py:72
  17.2 35.3 %collective-permute-start.2 = (bf16[64,4096]{1,0:T(8,128)(2,1)}, bf16[64,4096]{1,0:T(8,128)(2,1)}, u32[]{:S(2)}, u32[]{:S(2)}) collective-permute-start(bf16[64,4096]{1,0:T(8,128)(2,1)} %fusion.2), channel_id=1, source_target_pairs={{0,192},{1,193},{2,194},{3,195},{4,196},{5,197},{6,198},{7,199},{8... | collective-permute-start | bytes 1572872 | tf_op jit(solution)/shard_map/ppermute | solution.py:72
  18.6 21.0 %all-to-all-start = ((bf16[16,24,896]{2,1,0:T(8,128)(2,1)}), bf16[16,24,896]{2,1,0:T(8,128)(2,1)S(1)}, u32[]{:S(2)}, u32[]{:S(2)}) async-start(bf16[16,24,896]{2,1,0:T(8,128)(2,1)} %bitcast.3), calls=%async_computation | async-start | bytes 1376256 | tf_op jit(solution)/shard_map/all_to_all | solution.py:324
  27.6 25.0 %collective-permute-start = (bf16[736,256]{1,0:T(8,128)(2,1)}, bf16[736,256]{1,0:T(8,128)(2,1)}, u32[]{:S(2)}, u32[]{:S(2)}) collective-permute-start(bf16[736,256]{1,0:T(8,128)(2,1)} %pad_maximum_fusion.4), channel_id=1, source_target_pairs={{0,0},{1,1},{2,2},{3,3},{4,4},{5,5},{6,6},{7,7},{8,8},{9,9},{10,10... | collective-permute-start | bytes 1130504 | tf_op jit(solution)/shard_map/ppermute | solution.py:72
  52.5 24.1 %all-to-all-start.1 = ((bf16[16,16,896]{2,1,0:T(8,128)(2,1)}), bf16[16,16,896]{2,1,0:T(8,128)(2,1)S(1)}, u32[]{:S(2)}, u32[]{:S(2)}) async-start(bf16[16,16,896]{2,1,0:T(8,128)(2,1)} %bitcast.6), calls=%async_computation.1 | async-start | bytes 917504 | tf_op jit(solution)/shard_map/all_to_all | solution.py:330
  60.2 64.4 %all-gather.6.cloned.1.call-start = ((), (), s32[]{:S(2)}) async-start(), calls=%async_computation.3 | async-start | bytes 3391488 | tf_op jit(solution)/shard_map/all_gather | solution.py:334
  60.3 9.4 %collective-permute-start.3 = (bf16[736,256]{1,0:T(8,128)(2,1)}, bf16[736,256]{1,0:T(8,128)(2,1)S(1)}, u32[]{:S(2)}, u32[]{:S(2)}) collective-permute-start(bf16[736,256]{1,0:T(8,128)(2,1)} %collective-permute-done), channel_id=1, source_target_pairs={{0,0},{1,1},{2,18},{3,19},{4,68},{5,69},{6,86},{7,87},{8,136},{9,1... | collective-permute-start | bytes 1130504 | tf_op jit(solution)/shard_map/ppermute | solution.py:72
  69.7 7.0 %copy-start.6 = (bf16[736,256]{1,0:T(8,128)(2,1)}, bf16[736,256]{1,0:T(8,128)(2,1)S(1)}, u32[]{:S(2)}) copy-start(bf16[736,256]{1,0:T(8,128)(2,1)S(1)} %collective-permute-done.3) | copy-start | bytes 1130500
  76.7 101.8 %all-gather.8.cloned.1.call-start = ((), (), s32[]{:S(2)}) async-start(), calls=%async_computation.4 | async-start | bytes 4718592 | tf_op jit(solution)/shard_map/all_gather | solution.py:353
  76.7 13.8 %collective-permute-start.5 = (bf16[1792,896]{1,0:T(8,128)(2,1)}, bf16[1792,896]{1,0:T(8,128)(2,1)S(1)}, u32[]{:S(2)}, u32[]{:S(2)}) collective-permute-start(bf16[1792,896]{1,0:T(8,128)(2,1)} %all-gather.4.cloned.1.call-done), channel_id=1, source_target_pairs={{0,16},{1,17},{2,18},{3,19},{4,20},{5,21},{6,22},{7,23},{8,24},{9,... | collective-permute-start | bytes 9633800 | tf_op jit(solution)/shard_map/ppermute | solution.py:72
  77.3 13.2 %collective-permute-start.4 = (bf16[256,896]{1,0:T(8,128)(2,1)S(1)}, bf16[256,896]{1,0:T(8,128)(2,1)S(1)}, u32[]{:S(2)}, u32[]{:S(2)}) collective-permute-start(bf16[256,896]{1,0:T(8,128)(2,1)S(1)} %bitcast.31), channel_id=1, source_target_pairs={{0,1},{1,32},{2,3},{3,34},{4,5},{5,36},{6,7},{7,38},{8,9},{9,40},{... | collective-permute-start | bytes 1376264 | tf_op jit(solution)/shard_map/ppermute | solution.py:72
  79.5 11.1 %collective-permute-start.6 = (bf16[512,256]{1,0:T(8,128)(2,1)S(1)}, bf16[512,256]{1,0:T(8,128)(2,1)S(1)}, u32[]{:S(2)}, u32[]{:S(2)}) collective-permute-start(bf16[512,256]{1,0:T(8,128)(2,1)S(1)} %pad_maximum_fusion.5), channel_id=1, source_target_pairs={{0,0},{1,1},{2,2},{3,3},{4,4},{5,5},{6,6},{7,7},{8,8},{9,9},{10,10... | collective-permute-start | bytes 786440 | tf_op jit(solution)/shard_map/ppermute | solution.py:72
  90.6 15.1 %collective-permute-start.7 = (bf16[512,256]{1,0:T(8,128)(2,1)S(1)}, bf16[512,256]{1,0:T(8,128)(2,1)S(1)}, u32[]{:S(2)}, u32[]{:S(2)}) collective-permute-start(bf16[512,256]{1,0:T(8,128)(2,1)S(1)} %collective-permute-done.6), channel_id=1, source_target_pairs={{0,0},{1,1},{2,18},{3,19},{4,68},{5,69},{6,86},{7,87},{8,136},{9,1... | collective-permute-start | bytes 786440 | tf_op jit(solution)/shard_map/ppermute | solution.py:72
  98.0 1.9 copy-start.1
  105.7 9.2 %collective-permute-start.8 = (bf16[256,896]{1,0:T(8,128)(2,1)}, bf16[256,896]{1,0:T(8,128)(2,1)}, u32[]{:S(2)}, u32[]{:S(2)}) collective-permute-start(bf16[256,896]{1,0:T(8,128)(2,1)} %encode.2), channel_id=1, source_target_pairs={{0,33},{1,0},{2,35},{3,2},{4,37},{5,4},{6,39},{7,6},{8,41},{9,8},{... | collective-permute-start | bytes 1376264 | tf_op jit(solution)/shard_map/ppermute | solution.py:72
  107.4 6.1 %collective-permute-start.10 = (bf16[512,256]{1,0:T(8,128)(2,1)S(1)}, bf16[512,256]{1,0:T(8,128)(2,1)S(1)}, u32[]{:S(2)}, u32[]{:S(2)}) collective-permute-start(bf16[512,256]{1,0:T(8,128)(2,1)S(1)} %collective-permute-done.7), channel_id=1, source_target_pairs={{0,1},{1,32},{2,3},{3,34},{4,5},{5,36},{6,7},{7,38},{8,9},{9,40},{... | collective-permute-start | bytes 786440 | tf_op jit(solution)/shard_map/ppermute | solution.py:72
  108.4 14.4 %collective-permute-start.9 = (bf16[64,4096]{1,0:T(8,128)(2,1)}, bf16[64,4096]{1,0:T(8,128)(2,1)}, u32[]{:S(2)}, u32[]{:S(2)}) collective-permute-start(bf16[64,4096]{1,0:T(8,128)(2,1)} %fusion.2), channel_id=1, source_target_pairs={{0,128},{1,129},{2,130},{3,131},{4,132},{5,133},{6,134},{7,135},{8... | collective-permute-start | bytes 1572872 | tf_op jit(solution)/shard_map/ppermute | solution.py:72
  124.6 3.0 %copy-start.5 = (bf16[5888,256]{1,0:T(8,128)(2,1)S(1)}, bf16[5888,256]{1,0:T(8,128)(2,1)}, u32[]{:S(2)}) copy-start(bf16[5888,256]{1,0:T(8,128)(2,1)} %all-gather.6.cloned.1.call-done) | copy-start | bytes 9043972
  126.5 26.9 %collective-permute-start.12 = (bf16[256,4096]{1,0:T(8,128)(2,1)S(1)}, bf16[256,4096]{1,0:T(8,128)(2,1)S(1)}, u32[]{:S(2)}, u32[]{:S(2)}) collective-permute-start(bf16[256,4096]{1,0:T(8,128)(2,1)S(1)} %pad_maximum_fusion), channel_id=1, source_target_pairs={{0,16},{1,17},{2,18},{3,19},{4,20},{5,21},{6,22},{7,23},{8,24},{9,... | collective-permute-start | bytes 6291464 | tf_op jit(solution)/shard_map/ppermute | solution.py:72
  127.9 11.9 %collective-permute-start.18 = (bf16[256,896]{1,0:T(8,128)(2,1)S(1)}, bf16[256,896]{1,0:T(8,128)(2,1)S(1)}, u32[]{:S(2)}, u32[]{:S(2)}) collective-permute-start(bf16[256,896]{1,0:T(8,128)(2,1)S(1)} %add_convert_fusion.3.refs_1_), channel_id=1, source_target_pairs={{0,192},{1,193},{2,194},{3,195},{4,196},{5,197},{6,198},{7,199},{8... | collective-permute-start | bytes 1376264 | tf_op jit(solution)/shard_map/ppermute | solution.py:72
  129.0 12.8 %collective-permute-start.16 = (bf16[256,896]{1,0:T(8,128)(2,1)S(1)}, bf16[256,896]{1,0:T(8,128)(2,1)S(1)}, u32[]{:S(2)}, u32[]{:S(2)}) collective-permute-start(bf16[256,896]{1,0:T(8,128)(2,1)S(1)} %add_convert_fusion.3.refs_1_), channel_id=1, source_target_pairs={{0,128},{1,129},{2,130},{3,131},{4,132},{5,133},{6,134},{7,135},{8... | collective-permute-start | bytes 1376264 | tf_op jit(solution)/shard_map/ppermute | solution.py:72
  130.1 22.9 %collective-permute-start.14 = (bf16[256,896]{1,0:T(8,128)(2,1)S(1)}, bf16[256,896]{1,0:T(8,128)(2,1)S(1)}, u32[]{:S(2)}, u32[]{:S(2)}) collective-permute-start(bf16[256,896]{1,0:T(8,128)(2,1)S(1)} %add_convert_fusion.3.refs_1_), channel_id=1, source_target_pairs={{0,64},{1,65},{2,66},{3,67},{4,68},{5,69},{6,70},{7,71},{8,72},{9,... | collective-permute-start | bytes 1376264 | tf_op jit(solution)/shard_map/ppermute | solution.py:72
  130.3 31.7 %collective-permute-start.11 = (bf16[4096,256]{1,0:T(8,128)(2,1)S(1)}, bf16[4096,256]{1,0:T(8,128)(2,1)S(1)}, u32[]{:S(2)}, u32[]{:S(2)}) collective-permute-start(bf16[4096,256]{1,0:T(8,128)(2,1)S(1)} %bitcast.28), channel_id=1, source_target_pairs={{0,1},{1,32},{2,3},{3,34},{4,5},{5,36},{6,7},{7,38},{8,9},{9,40},{... | collective-permute-start | bytes 6291464 | tf_op jit(solution)/shard_map/ppermute | solution.py:72
  139.8 25.7 %collective-permute-start.20 = (bf16[1792,256]{1,0:T(8,128)(2,1)S(1)}, bf16[1792,256]{1,0:T(8,128)(2,1)S(1)}, u32[]{:S(2)}, u32[]{:S(2)}) collective-permute-start(bf16[1792,256]{1,0:T(8,128)(2,1)S(1)} %pad_maximum_fusion.1.refs_3_), channel_id=1, source_target_pairs={{0,1},{1,32},{2,3},{3,34},{4,5},{5,36},{6,7},{7,38},{8,9},{9,40},{... | collective-permute-start | bytes 2752520 | tf_op jit(solution)/shard_map/ppermute | solution.py:72
  141.8 11.5 %collective-permute-start.19 = (bf16[256,896]{1,0:T(8,128)(2,1)S(1)}, bf16[256,896]{1,0:T(8,128)(2,1)S(1)}, u32[]{:S(2)}, u32[]{:S(2)}) collective-permute-start(bf16[256,896]{1,0:T(8,128)(2,1)S(1)} %collective-permute-done.18.refs_1_), channel_id=1, source_target_pairs={{0,16},{1,17},{2,18},{3,19},{4,20},{5,21},{6,22},{7,23},{8,24},{9,... | collective-permute-start | bytes 1376264 | tf_op jit(solution)/shard_map/ppermute | solution.py:72
  152.9 7.4 %collective-permute-start.13 = (bf16[256,896]{1,0:T(8,128)(2,1)S(1)}, bf16[256,896]{1,0:T(8,128)(2,1)S(1)}, u32[]{:S(2)}, u32[]{:S(2)}) collective-permute-start(bf16[256,896]{1,0:T(8,128)(2,1)S(1)} %add_convert_fusion.3.refs_1_), channel_id=1, source_target_pairs={{0,16},{1,17},{2,18},{3,19},{4,20},{5,21},{6,22},{7,23},{8,24},{9,... | collective-permute-start | bytes 1376264 | tf_op jit(solution)/shard_map/ppermute | solution.py:72
  153.3 3.7 %collective-permute-start.17 = (bf16[256,896]{1,0:T(8,128)(2,1)S(1)}, bf16[256,896]{1,0:T(8,128)(2,1)S(1)}, u32[]{:S(2)}, u32[]{:S(2)}) collective-permute-start(bf16[256,896]{1,0:T(8,128)(2,1)S(1)} %collective-permute-done.16.refs_1_), channel_id=1, source_target_pairs={{0,16},{1,17},{2,18},{3,19},{4,20},{5,21},{6,22},{7,23},{8,24},{9,... | collective-permute-start | bytes 1376264 | tf_op jit(solution)/shard_map/ppermute | solution.py:72
  153.4 5.2 %collective-permute-start.15 = (bf16[256,896]{1,0:T(8,128)(2,1)S(1)}, bf16[256,896]{1,0:T(8,128)(2,1)S(1)}, u32[]{:S(2)}, u32[]{:S(2)}) collective-permute-start(bf16[256,896]{1,0:T(8,128)(2,1)S(1)} %collective-permute-done.14.refs_1_), channel_id=1, source_target_pairs={{0,16},{1,17},{2,18},{3,19},{4,20},{5,21},{6,22},{7,23},{8,24},{9,... | collective-permute-start | bytes 1376264 | tf_op jit(solution)/shard_map/ppermute | solution.py:72
  178.5 2.2 copy-start.2
  183.9 31.7 %copy-start.4 = (bf16[64,4096]{1,0:T(8,128)(2,1)S(1)}, bf16[64,4096]{1,0:T(8,128)(2,1)}, u32[]{:S(2)}) copy-start(bf16[64,4096]{1,0:T(8,128)(2,1)} %param.9) | copy-start | bytes 1572868
  184.0 4.5 %collective-permute-start.21 = (bf16[256,4096]{1,0:T(8,128)(2,1)S(1)}, bf16[256,4096]{1,0:T(8,128)(2,1)S(1)}, u32[]{:S(2)}, u32[]{:S(2)}) collective-permute-start(bf16[256,4096]{1,0:T(8,128)(2,1)S(1)} %get-tuple-element.84), channel_id=1, source_target_pairs={{0,16},{1,17},{2,18},{3,19},{4,20},{5,21},{6,22},{7,23},{8,24},{9,... | collective-permute-start | bytes 6291464 | tf_op jit(solution)/shard_map/ppermute | solution.py:72
  188.9 14.8 %collective-permute-start.22 = (bf16[64,4096]{1,0:T(8,128)(2,1)S(1)}, bf16[64,4096]{1,0:T(8,128)(2,1)S(1)}, u32[]{:S(2)}, u32[]{:S(2)}) collective-permute-start(bf16[64,4096]{1,0:T(8,128)(2,1)S(1)} %get-tuple-element.87), channel_id=1, source_target_pairs={{0,128},{1,129},{2,130},{3,131},{4,132},{5,133},{6,134},{7,135},{8... | collective-permute-start | bytes 1572872 | tf_op jit(solution)/shard_map/ppermute | solution.py:72
  191.7 23.3 %collective-permute-start.23 = (bf16[64,4096]{1,0:T(8,128)(2,1)S(1)}, bf16[64,4096]{1,0:T(8,128)(2,1)S(1)}, u32[]{:S(2)}, u32[]{:S(2)}) collective-permute-start(bf16[64,4096]{1,0:T(8,128)(2,1)S(1)} %get-tuple-element.89), channel_id=1, source_target_pairs={{0,192},{1,193},{2,194},{3,195},{4,196},{5,197},{6,198},{7,199},{8... | collective-permute-start | bytes 1572872 | tf_op jit(solution)/shard_map/ppermute | solution.py:72
  192.6 23.0 %collective-permute-start.24 = (bf16[64,4096]{1,0:T(8,128)(2,1)S(1)}, bf16[64,4096]{1,0:T(8,128)(2,1)S(1)}, u32[]{:S(2)}, u32[]{:S(2)}) collective-permute-start(bf16[64,4096]{1,0:T(8,128)(2,1)S(1)} %get-tuple-element.88), channel_id=1, source_target_pairs={{0,64},{1,65},{2,66},{3,67},{4,68},{5,69},{6,70},{7,71},{8,72},{9,... | collective-permute-start | bytes 1572872 | tf_op jit(solution)/shard_map/ppermute | solution.py:72
Sparse Core Ops, SparseCore 0:
  9.1 67.2 all-gather.3
  78.2 46.3 all-gather.5
  126.4 52.0 all-gather.7
